TPU v7x, 512 devices: a whole 4x8x8 slice. The times are simulated.
512 devices in a mesh: dp: 32 (over y, x), vocab: 16 (over z, core).
Axes of the slice: x: 4, y: 8, z: 8, core: 2. Of those that a mesh axis runs over, the one named last changes fastest.
Arguments:
- hidden: bfloat16 [256, 4608], P('dp'), may hold values from -6 to 6
- labels: int32 [256], replicated, may hold values from 0 to 255999
- head_weight: bfloat16 [256000, 4608], P(('dp', 'vocab')), may hold values from -1 to 1
- factor_rows: float32 [4608, 4608], P(('dp', 'vocab')), may hold values from -0.0002 to 16, as said below
Outputs:
- new_factor: float32 [4608, 4608], P(('dp', 'vocab'))
- gradients: bfloat16 [256, 4608], P('dp', 'vocab')
Inputs may be any that keep to these rules, and one draw needn't show every extreme that they name: factor_rows is symmetric and positive definite.
All inputs are finite; a program needn't handle non-finite values.
Results may differ from a plain program's by a relative error of at most 0.0037.
Values may be sent and summed in bfloat16 or wider, within the bound.
A program may use at most 64 MiB of HBM per device.

v0:
```python
import jax
import jax.numpy as jnp
from jax import lax
from jax.sharding import PartitionSpec as P

softcap = 30.0
decay_rate = 0.95


def on_device(hidden, labels, head_weight, factor_rows):
    gathered = lax.all_gather(hidden, "dp", axis=0, tiled=True)
    raw_logits = jnp.einsum("td,vd->tv", gathered, head_weight, preferred_element_type=jnp.float32)
    squash = jnp.tanh(raw_logits / softcap)
    exp_terms = jnp.exp(softcap * squash)
    denominator = lax.psum(jnp.sum(exp_terms, axis=1), ("dp", "vocab"))
    vocab_rows = head_weight.shape[0]
    flat_index = lax.axis_index("dp") * lax.axis_size("vocab") + lax.axis_index("vocab")
    offset = labels - flat_index * vocab_rows
    onehot = (lax.broadcasted_iota(jnp.int32, raw_logits.shape, 1) == offset[:, None]).astype(
        jnp.float32
    )
    logit_grad = ((exp_terms / denominator[:, None] - onehot) * (1.0 - squash * squash)).astype(
        jnp.bfloat16
    )
    partial_value = jnp.dot(logit_grad, head_weight, preferred_element_type=jnp.float32)
    row_count = factor_rows.shape[0]
    summed = lax.psum(partial_value, ("dp", "vocab"))
    gradients = summed.astype(jnp.bfloat16)
    own_columns = lax.dynamic_slice_in_dim(gradients, flat_index * row_count, row_count, 1)
    gram_rows = lax.dot_general(
        own_columns, gradients, (((0,), (0,)), ((), ())), preferred_element_type=jnp.float32
    )
    model_width = hidden.shape[1]
    token_count = gathered.shape[0]
    new_factor = (
        decay_rate * factor_rows + (1.0 - decay_rate) * (model_width / token_count) * gram_rows
    )
    own_tokens = hidden.shape[0]
    column_width = model_width // lax.axis_size("vocab")
    grad_block = lax.dynamic_slice(
        gradients,
        (lax.axis_index("dp") * own_tokens, lax.axis_index("vocab") * column_width),
        (own_tokens, column_width),
    )
    return (new_factor, grad_block)


def solution(mesh):
    placed = (P("dp", None), P(), P(("dp", "vocab"), None), P(("dp", "vocab"), None))
    return jax.shard_map(
        on_device,
        mesh=mesh,
        in_specs=placed,
        out_specs=(P(("dp", "vocab"), None), P("dp", "vocab")),
        check_vma=False,
    )
```

profile of v0, /device:TPU:1, one launch (start us, length us, event | category | flops | bytes accessed | tf_op | source)
XLA Modules:
  0.0 327.9 jit_solution(30174645308936239)
XLA Ops:
  7.2 0.0 all-gather.2.cloned.1.call-start
  7.2 0.7 all-gather.2.cloned.1.call-update
  7.9 0.7 broadcast_subtract_fusion
  8.6 87.9 %all-gather.2.cloned.1.call-done = bf16[256,4608]{1,0:T(8,128)(2,1)} async-done(((bf16[8,4608]{1,0:T(8,128)(2,1)}), bf16[256,4608]{1,0:T(8,128)(2,1)}) %all-gather.2.cloned.1.call-update) | async-done | bytes 2359312 | tf_op jit(solution)/shard_map/all_gather | solution.py:11
  96.4 4.5 %fusion.2 = (f32[256]{0:T(256)S(1)}, f32[256,500]{0,1:T(8,128)S(1)}) fusion(bf16[256,4608]{1,0:T(8,128)(2,1)} %all-gather.2.cloned.1.call-done, bf16[500,4608]{1,0:T(8,128)(2,1)} %param.6), kind=kOutput, calls=%fused_computation.7 | convolution fusion | flops 1180031744 | bytes 7480320 | tf_op jit(solution)/shard_map/td,vd->tv/dot_general | solution.py:12
  100.9 100.0 %psum.14 = f32[256]{0:T(256)S(1)} all-reduce(f32[256]{0:T(256)S(1)} %get-tuple-element.2), channel_id=1, replica_groups=mesh['dp'=32,'vocab'=16] {'dp','vocab'}, use_global_device_ids=true, to_apply=%region_1.0 | all-reduce | flops 256 | bytes 2048 | tf_op jit(solution)/shard_map/psum | solution.py:15
  201.0 5.9 %fusion.3 = f32[256,4608]{1,0:T(8,128)} fusion(bf16[500,4608]{1,0:T(8,128)(2,1)} %param.6, f32[256,500]{0,1:T(8,128)S(1)} %get-tuple-element.3, s32[256]{0:T(256)S(1)} %broadcast_subtract_fusion, f32[256]{0:T(256)S(1)} %psum.14), kind=kOutput, calls=%fused_computation.8 | convolution fusion | flops 1180800000 | bytes 9840640 | tf_op jit(solution)/shard_map/dot_general | solution.py:25
  206.9 0.0 copy-start
  206.9 112.3 %all-reduce.1 = bf16[256,4608]{1,0:T(8,128)(2,1)S(1)} all-reduce(f32[256,4608]{1,0:T(8,128)} %fusion.3), channel_id=1, replica_groups=mesh['dp'=32,'vocab'=16] {'dp','vocab'}, use_global_device_ids=true, to_apply=%region_2.0 | all-reduce | flops 1179648 | bytes 7077888 | tf_op jit(solution)/shard_map/psum | solution.py:27
  319.2 0.7 dynamic_slice.7
  319.9 0.0 copy-done
  319.9 1.2 fusion
Async XLA Ops:
  7.2 89.3 %all-gather.2.cloned.1.call-start = ((), (), s32[]{:S(2)}) async-start(), calls=%async_computation | async-start | bytes 2433024 | tf_op jit(solution)/shard_map/all_gather | solution.py:11
  206.9 113.0 %copy-start = (f32[9,4608]{1,0:T(8,128)S(1)}, f32[9,4608]{1,0:T(8,128)}, u32[]{:S(2)}) copy-start(f32[9,4608]{1,0:T(8,128)} %param.7) | copy-start | bytes 497668
Sparse Core Ops, SparseCore 0:
  11.2 85.2 all-gather.1
where the time goes:
time: 328 us
  blocking collectives  212 us (65%)
  waiting for transfers between devices  88.5 us (27%)
  between operations  14.1 us (4%)
  matrix products  11.6 us (4%)
    psum x1, blocking collectives, on_device(): summed = lax.psum(partial_value, ('dp', 'vocab'))  112 us
    psum x1, blocking collectives, on_device(): denominator = lax.psum(jnp.sum(exp_terms, axis=1), ('dp', 'vocab'))  100 us
    all_gather x1, waiting for transfers between devices, on_device(): gathered = lax.all_gather(hidden, 'dp', axis=0, tiled=True)  87.9 us
  transfers between devices with their start and end apart: 1, of which 1 were waited for; matrix products, arithmetic and copies ran while one was open for 0% of the time, Pallas kernels for 0%

commit v1 on v0

v1 whole, which is shorter than its diff:
```python
import jax
import jax.numpy as jnp
from jax import lax
from jax.experimental import pallas as pl
from jax.experimental.pallas import tpu as pltpu
from jax.sharding import PartitionSpec as P

softcap = 30.0
decay_rate = 0.95

NX, NY, NZ, NC = 4, 8, 8, 2
PLANE, LINE = NX * NY, NZ * NC
D, TOKENS, ROWS = 4608, 256, 500
PADDED = 512
HALF = D // 2
CHUNK = D // LINE
UNITS = CHUNK // 8 // NX
XU = 6
MESH = pl.DeviceIdType.MESH
f32, bf16 = jnp.float32, jnp.bfloat16


def kernel(
    hidden, labels, head, factor, new_factor, grads,
    wv, wt, hb, h2, lt, ds_, dr_, px, pz, rx, rz, qx, qz, r2x, r2z, ry, gb, rb, tb, rt, den_a, den_b,
    w_sem, hs, hr, hds, hdr, das, dar, dbs, dbr, c_s, c_r, xs, xr, zs, zr, x2s, x2r, z2s, z2r,
    ys, yr, gs, gr, bs, br, ts, tr,
):
    dp, vo = lax.axis_index("dp"), lax.axis_index("vocab")
    x, y = lax.rem(dp, NX), dp // NX
    c, z = lax.rem(vo, NC), vo // NC
    sib = vo + 1 - 2 * c

    def copy(src, dst, send, recv, to_dp, to_vo):
        return pltpu.make_async_remote_copy(
            src_ref=src, dst_ref=dst, send_sem=send, recv_sem=recv, device_id=(to_dp, to_vo), device_id_type=MESH
        )

    def got(ref, recv):
        copy(ref, ref, recv, recv, dp, sib).wait_recv()

    def sent(ref, send):
        copy(ref, ref, send, send, dp, sib).wait_send()

    def each(count, body):
        lax.fori_loop(1, count, lambda k, carry: (body(k), carry)[1], 0)

    def xp(k):
        return lax.rem(x + k, NX)

    def yp(k):
        return lax.rem(y + k + NY, NY)

    def zp(k):
        return lax.rem(z + k, NZ)

    def at_x(k):
        return y * NX + xp(k)

    def at_y(k):
        return yp(k) * NX + x

    def at_z(k):
        return zp(k) * NC + c

    w_copy = pltpu.make_async_copy(head, wv, w_sem)
    w_copy.start()
    gb[...] = jnp.zeros_like(gb)
    wt[:, PADDED - 128:] = jnp.zeros((D, 128), bf16)
    lt[PADDED - 16:, :] = jnp.zeros((16, TOKENS), bf16)

    barrier = pltpu.get_barrier_semaphore()
    each(LINE, lambda k: pl.semaphore_signal(
        barrier, inc=1, device_id=(dp, lax.rem(vo + k, LINE)), device_id_type=MESH))
    each(PLANE, lambda k: pl.semaphore_signal(
        barrier, inc=1, device_id=(lax.rem(dp + k, PLANE), vo), device_id_type=MESH))
    pl.semaphore_wait(barrier, LINE + PLANE - 2)

    def transpose_head(first, last):
        def body(b, carry):
            at = pl.multiple_of(b * 256, 256)
            wt[pl.ds(at, 256), 0:ROWS] = wv[:, pl.ds(at, 256)].T
            return carry

        lax.fori_loop(first, last, body, 0)

    @pl.when(c == 0)
    def _():
        hb[0, dp] = hidden[:, 0:HALF]
        for k in (1, 2, 3):
            copy(hb.at[0, dp], hb.at[0, dp], hs.at[k], hr.at[dp], at_x(k), vo).start()
        w_copy.wait()
        transpose_head(0, 6)
        for k in (1, 2, 3):
            got(hb.at[0, at_x(k)], hr.at[at_x(k)])

        def row(k):
            return hb.at[0, pl.ds(yp(k) * NX, NX)]

        def row_copy(from_k, to_k, sem):
            return copy(row(from_k), row(from_k), hs.at[sem], hr.at[yp(from_k) * NX], at_y(to_k), vo)

        def across(k):
            copy(row(k), row(k), hds.at[yp(k)], hdr.at[yp(k)], dp, sib).start()

        def row_got(k):
            got(row(k), hr.at[yp(k) * NX])

        row_copy(0, 1, 4).start()
        row_copy(0, -1, 5).start()
        row_copy(0, 4, 6).start()
        across(0)
        transpose_head(6, 12)
        row_got(-1)
        row_copy(-1, 1, 7).start()
        row_got(1)
        row_copy(1, -1, 8).start()
        across(-1)
        across(1)
        transpose_head(12, 18)
        row_got(4)
        row_copy(4, 1, 9).start()
        row_copy(4, -1, 10).start()
        across(4)
        for k in (2, -2, 3, -3):
            row_got(k)
            across(k)
        for k in (1, 2, 3):
            sent(hb.at[0, dp], hs.at[k])
        for sem in range(4, 11):
            sent(row(0), hs.at[sem])

    @pl.when(c == 1)
    def _():
        hb[1, dp] = hidden[:, HALF:]

        def own(k):
            return hb.at[1, at_y(k)]

        def spread(k):
            for i in (1, 2, 3):
                copy(own(k), own(k), hs.at[7 + yp(k) * 3 + i], hr.at[at_y(k)], yp(0) * NX + xp(i), vo).start()

        for k in (1, -1, 2, -2, 3, -3, 4):
            copy(own(0), own(0), hs.at[yp(k)], hr.at[dp], at_y(k), vo).start()
        spread(0)
        w_copy.wait()
        transpose_head(0, 12)
        for k in (1, -1, 2, -2, 3, -3, 4):
            got(own(k), hr.at[at_y(k)])
            spread(k)
        transpose_head(12, 18)

        def across(v, carry):
            for i in (1, 2, 3):
                slot = v * NX + xp(i)
                got(hb.at[1, slot], hr.at[slot])
            rows = hb.at[1, pl.ds(v * NX, NX)]
            copy(rows, rows, hds.at[v], hdr.at[v], dp, sib).start()
            return carry

        lax.fori_loop(0, NY, across, 0)
        for k in (1, -1, 2, -2, 3, -3, 4):
            sent(own(0), hs.at[yp(k)])
        for k in range(8, 32):
            sent(own(0), hs.at[k])

    def across_done(v, carry):
        got(hb.at[1 - c, pl.ds(v * NX, NX)], hdr.at[v])
        sent(hb.at[c, pl.ds(v * NX, NX)], hds.at[v])
        return carry

    lax.fori_loop(0, NY, across_done, 0)

    raw = jnp.zeros((ROWS, TOKENS), f32)
    for h in range(2):
        for part in range(2):
            width = HALF // 2
            h2[...] = hb[h, :, :, part * width:(part + 1) * width].astype(f32).reshape(TOKENS, width).astype(bf16)
            at = h * HALF + part * width
            raw += lax.dot_general(
                wv[:, at:at + width], h2[...], (((1,), (1,)), ((), ())), preferred_element_type=f32)
    squash = jnp.tanh(raw * (1.0 / softcap))
    terms = jnp.exp(softcap * squash)

    den_a[vo] = jnp.sum(terms, axis=0, keepdims=True)
    each(LINE, lambda k: copy(
        den_a.at[vo], den_a.at[vo], das.at[k], dar.at[vo], dp, lax.rem(vo + k, LINE)).start())
    each(LINE, lambda k: got(den_a.at[vo], dar.at[lax.rem(vo + k, LINE)]))
    each(LINE, lambda k: sent(den_a.at[vo], das.at[k]))
    den_b[dp] = jnp.sum(den_a[...], axis=0)
    each(PLANE, lambda k: copy(
        den_b.at[dp], den_b.at[dp], dbs.at[k], dbr.at[dp], lax.rem(dp + k, PLANE), vo).start())
    each(PLANE, lambda k: got(den_b.at[dp], dbr.at[lax.rem(dp + k, PLANE)]))
    each(PLANE, lambda k: sent(den_b.at[dp], dbs.at[k]))
    denominator = jnp.sum(den_b[...], axis=0)

    onehot = lax.broadcasted_iota(jnp.int32, (ROWS, TOKENS), 0) == labels[...] - (dp * LINE + vo) * ROWS
    lt[0:ROWS, :] = (
        (terms * (1.0 / denominator) - onehot.astype(f32)) * (1.0 - squash * squash)).astype(bf16)

    def partial_of(i, core):
        start = pl.multiple_of((i * NC + core) * CHUNK, 32)
        product = jnp.dot(wt[pl.ds(start, CHUNK), :], lt[...], preferred_element_type=f32)
        return product.reshape(NX, UNITS, 8, TOKENS)

    def first(i, carry):
        ds_[i] = partial_of(i, 1 - c).astype(bf16)
        copy(ds_.at[i], dr_.at[i], c_s.at[i], c_r.at[i], dp, sib).start()
        return carry

    lax.fori_loop(0, NZ, first, 0)
    for g in range(2):
        def second(i, carry, g=g):
            total = partial_of(i, c)
            got(dr_.at[i], c_r.at[i])
            total = (total + dr_[i].astype(f32)).astype(bf16)
            for v in range(NX):
                px[g, v, i - 4 * g] = total[v, 0:XU]
                pz[i, v] = total[v, XU:]

            @pl.when(i != z)
            def _():
                copy(pz.at[i], rz.at[z], zs.at[i], zr.at[z], dp, i * NC + c).start()

            return carry

        lax.fori_loop(4 * g, 4 * g + 4, second, 0)
        for k in (1, 2, 3):
            copy(px.at[g, xp(k)], rx.at[g, x], xs.at[g, k], xr.at[g, x], at_x(k), vo).start()

    each(NZ, lambda k: got(rz.at[0], zr.at[zp(k)]))
    total = pz[z].astype(f32)
    for k in range(1, NZ):
        total += rz[zp(k)].astype(f32)
    qz[...] = total.astype(bf16)
    for k in (1, 2, 3):
        copy(qz.at[xp(k)], r2z.at[x], z2s.at[k], z2r.at[x], at_x(k), vo).start()
    for g in range(2):
        total = px[g, x].astype(f32)
        for k in (1, 2, 3):
            got(rx.at[g, 0], xr.at[g, xp(k)])
            total += rx[g, xp(k)].astype(f32)
        qx[4 * g:4 * g + 4] = total.astype(bf16)
    each(NZ, lambda k: copy(
        qx.at[zp(k)], r2x.at[z], x2s.at[k], x2r.at[z], dp, at_z(k)).start())
    total = qz[x].astype(f32)
    for k in (1, 2, 3):
        got(r2z.at[0], z2r.at[xp(k)])
        total += r2z[xp(k)].astype(f32)
    ry[y, XU:] = total.astype(bf16)
    each(NZ, lambda k: got(r2x.at[0], x2r.at[zp(k)]))
    total = qx[z].astype(f32)
    for k in range(1, NZ):
        total += r2x[zp(k)].astype(f32)
    ry[y, 0:XU] = total.astype(bf16)

    each(NY, lambda k: copy(ry.at[y], ry.at[y], ys.at[k], yr.at[y], at_y(k), vo).start())
    each(NY, lambda k: got(ry.at[0], yr.at[yp(k)]))
    each(NY, lambda k: sent(ry.at[0], ys.at[k]))
    total = ry[0].astype(f32)
    for k in range(1, NY):
        total += ry[k].astype(f32)
    shift = lax.rem(vo, 4) * 4

    def quarter(v):
        return gb.at[pl.ds(shift + v * UNITS, UNITS)]

    gb[pl.ds(shift + x * UNITS, UNITS)] = total.astype(bf16)
    for k in (1, 2, 3):
        copy(quarter(x), quarter(x), gs.at[k], gr.at[x], at_x(k), vo).start()
    for k in (1, 2, 3):
        got(quarter(xp(k)), gr.at[xp(k)])
    for k in (1, 2, 3):
        sent(quarter(x), gs.at[k])

    source = y * NC + x // 2
    own_rows = gb.at[pl.ds(shift + lax.rem(x, 2) * 18, 18)]

    @pl.when(vo == source)
    def _():
        each(LINE, lambda k: copy(own_rows, rb, bs.at[k], br, dp, lax.rem(vo + k, LINE)).start())
        rb[...] = gb[pl.ds(shift + lax.rem(x, 2) * 18, 18)]
        each(LINE, lambda k: sent(rb, bs.at[k]))

    @pl.when(vo != source)
    def _():
        got(rb, br)

    rows = rb[...].astype(f32).reshape(144, TOKENS).astype(bf16)
    line_row = lax.broadcasted_iota(jnp.int32, (256, 144), 0)
    column = lax.broadcasted_iota(jnp.int32, (256, 144), 1)
    place, within = line_row // 16, lax.rem(line_row, 16)
    pick = jnp.where((within < 9) & (column == place * 9 + within), 1.0, 0.0).astype(bf16)
    spread_rows = jnp.dot(pick, rows, preferred_element_type=f32).astype(bf16)
    columns = gb[...].astype(f32).reshape(384, TOKENS).astype(bf16)
    gram = lax.dot_general(spread_rows, columns, (((1,), (1,)), ((), ())), preferred_element_type=f32)
    tb[...] = gram.reshape(LINE, 16, 384).astype(bf16)
    each(LINE, lambda k: copy(
        tb.at[lax.rem(vo + k, LINE)], rt.at[vo], ts.at[k], tr.at[vo], dp, lax.rem(vo + k, LINE)).start())

    block = gb[pl.ds(shift, 36)].astype(f32).reshape(CHUNK, TOKENS).astype(bf16)
    token = lax.broadcasted_iota(jnp.int32, (8, TOKENS), 1)
    mine = jnp.where(token == dp * 8 + lax.broadcasted_iota(jnp.int32, (8, TOKENS), 0), 1.0, 0.0).astype(bf16)
    grads[...] = lax.dot_general(
        mine, block, (((1,), (1,)), ((), ())), preferred_element_type=f32).astype(bf16)

    new_factor[...] = decay_rate * factor[...]
    rt[vo] = tb[vo]
    each(LINE, lambda k: got(rt.at[0], tr.at[lax.rem(vo + k, LINE)]))
    scale = (1.0 - decay_rate) * (D / TOKENS)
    for v in range(LINE):
        at = v * CHUNK // 128 * 128
        new_factor[:, at:at + 384] += scale * rt[v].astype(f32)[0:9]

    each(NZ, lambda k: sent(pz.at[0], zs.at[zp(k)]))
    each(NZ, lambda k: sent(qx.at[0], x2s.at[k]))
    for k in (1, 2, 3):
        sent(qz.at[0], z2s.at[k])
        for g in range(2):
            sent(px.at[g, 0], xs.at[g, k])
    lax.fori_loop(0, NZ, lambda i, carry: (sent(ds_.at[i], c_s.at[i]), carry)[1], 0)
    each(LINE, lambda k: sent(tb.at[0], ts.at[k]))


def on_device(hidden, labels, head_weight, factor_rows):
    vmem = pl.BlockSpec(memory_space=pltpu.VMEM)
    dma = pltpu.SemaphoreType.DMA

    def buf(*shape, dtype=bf16):
        return pltpu.VMEM(shape, dtype)

    return pl.pallas_call(
        kernel,
        out_shape=(
            jax.ShapeDtypeStruct(factor_rows.shape, f32),
            jax.ShapeDtypeStruct((TOKENS // PLANE, CHUNK), bf16),
        ),
        in_specs=[vmem, vmem, pl.BlockSpec(memory_space=pl.ANY), vmem],
        out_specs=(vmem, vmem),
        scratch_shapes=[
            buf(ROWS, D), buf(D, PADDED), buf(2, PLANE, 8, HALF), buf(TOKENS, HALF // 2), buf(PADDED, TOKENS),
            buf(NZ, NX, UNITS, 8, TOKENS), buf(NZ, NX, UNITS, 8, TOKENS),
            buf(2, NX, 4, XU, 8, TOKENS), buf(NZ, NX, UNITS - XU, 8, TOKENS),
            buf(2, NX, 4, XU, 8, TOKENS), buf(NZ, NX, UNITS - XU, 8, TOKENS),
            buf(NZ, XU, 8, TOKENS), buf(NX, UNITS - XU, 8, TOKENS),
            buf(NZ, XU, 8, TOKENS), buf(NX, UNITS - XU, 8, TOKENS),
            buf(NY, UNITS, 8, TOKENS), buf(48, 8, TOKENS), buf(18, 8, TOKENS),
            buf(LINE, 16, 384), buf(LINE, 16, 384),
            buf(LINE, 1, TOKENS, dtype=f32), buf(PLANE, 1, TOKENS, dtype=f32),
            dma, dma((32,)), dma((32,)), dma((8,)), dma((8,)),
            dma((LINE,)), dma((LINE,)), dma((PLANE,)), dma((PLANE,)), dma((NZ,)), dma((NZ,)),
            dma((2, NX)), dma((2, NX)), dma((NZ,)), dma((NZ,)), dma((NZ,)), dma((NZ,)), dma((NX,)), dma((NX,)),
            dma((NY,)), dma((NY,)), dma((NX,)), dma((NX,)), dma((LINE,)), dma, dma((LINE,)), dma((LINE,)),
        ],
        compiler_params=pltpu.CompilerParams(
            collective_id=0, has_side_effects=True, vmem_limit_bytes=56 * 2**20),
        cost_estimate=pl.CostEstimate(flops=4 * 500 * 256 * 4608, bytes_accessed=6 * 2**20, transcendentals=2 * 500 * 256),
    )(hidden, labels.reshape(1, TOKENS), head_weight, factor_rows)


def solution(mesh):
    placed = (P("dp", None), P(), P(("dp", "vocab"), None), P(("dp", "vocab"), None))
    return jax.shard_map(
        on_device,
        mesh=mesh,
        in_specs=placed,
        out_specs=(P(("dp", "vocab"), None), P("dp", "vocab")),
        check_vma=False,
    )
```

time: 328 us -> 109 us (0.33)
  blocking collectives: 212 us -> 0 us
  Pallas kernels: 0 us -> 106 us
  waiting for transfers between devices: 88.5 us -> 0 us
  between operations: 14.1 us -> 0.64 us
  matrix products: 11.6 us -> 0 us
    psum x2 -> x0, blocking collectives: 212 us -> none  [the longest x1 112 us: on_device(): summed = lax.psum(partial_value, ('dp', 'vocab'))]
    pallas_call x0 -> x1, Pallas kernels: none -> 106 us  [on_device(): pl.pallas_call(kernel, out_shape=(jax.ShapeDtypeStruct(factor_rows.shape,...]
    all_gather x1 -> x0, waiting for transfers between devices: 87.9 us -> none  [on_device(): gathered = lax.all_gather(hidden, 'dp', axis=0, tiled=True)]
    dot_general x3 -> x0, matrix products: 11.6 us -> none  [the longest x1 5.93 us: on_device(): jnp.dot(logit_grad, head_weight, preferred_element_type=jnp.float32)]
  transfers between devices with their start and end apart: 1 -> 0, of which waited for: 1 -> 0; matrix products, arithmetic and copies ran while one was open for 0% -> 0% of each run, Pallas kernels for 0% -> 0%
where the time goes in v1:
time: 109 us
  Pallas kernels  106 us (97%)
  local copies, waits for them, and re-layouts  2.98 us (3%)
    pallas_call x1, Pallas kernels, on_device(): pl.pallas_call(kernel, out_shape=(jax.ShapeDtypeStruct(factor_rows.shape,...  106 us
    unnamed x2, local copies, waits for them, and re-layouts  2.98 us

profile of v1, /device:TPU:1, one launch (start us, length us, event | category | flops | bytes accessed | tf_op | source)
XLA Modules:
  0.0 109.2 jit_solution(6190018639374650941)
XLA Ops:
  0.6 105.6 %shard_map.59 = (f32[9,4608]{1,0:T(8,128)}, bf16[8,288]{1,0:T(8,128)(2,1)}) custom-call(bf16[8,4608]{1,0:T(8,128)(2,1)} %hidden.1, s32[1,256]{1,0:T(1,128)} %bitcast.1, bf16[500,4608]{1,0:T(8,128)(2,1)} %head.1, f32[9,4608]{1,0:T(8,128)} %factor.1), custom_call_target="tpu_custom_call" | custom-call | flops 2359296000 | bytes 6291456 | tf_op jit(solution)/shard_map/pallas_call | solution.py:333
  106.3 1.7 %copy.8 = f32[9,4608]{1,0:T(8,128)} copy(f32[9,4608]{1,0:T(8,128)} %get-tuple-element.4) | data formatting | bytes 331776
  108.0 1.3 %copy.9 = bf16[8,288]{1,0:T(8,128)(2,1)} copy(bf16[8,288]{1,0:T(8,128)(2,1)} %get-tuple-element.5) | data formatting | bytes 9216

commit v2 on v1

v2 whole, which is shorter than its diff:
```python
import jax
import jax.numpy as jnp
from jax import lax
from jax.experimental import pallas as pl
from jax.experimental.pallas import tpu as pltpu
from jax.sharding import PartitionSpec as P

softcap = 30.0
decay_rate = 0.95

NX, NY, NZ, NC = 4, 8, 8, 2
PLANE, LINE = NX * NY, NZ * NC
D, TOKENS, ROWS = 4608, 256, 500
PADDED = 512
SHARE = D // 3
CHUNK = D // LINE
UNITS = CHUNK // 8 // NX
XU = 6
MESH = pl.DeviceIdType.MESH
f32, bf16 = jnp.float32, jnp.bfloat16


def kernel(
    hidden, labels, head, factor, new_factor, grads,
    wv, wt, hb0, hb1, h2, lt, ds_, dr_, px, pz, rx, rz, qx, qz, r2x, r2z, ry, gb, rb, tb, rt, den_a, den_b, lab, bds, bdr, bpx, bpz, brx, brz,
    w_sem, hs, hr, hds, hdr, das, dar, dbs, dbr, c_s, c_r, xs, xr, zs, zr, x2s, x2r, z2s, z2r,
    ys, yr, gs, gr, bs, br, ts, tr, gds, gdr, bc_s, bc_r, bxs, bxr, bzs, bzr,
):
    dp, vo = lax.axis_index("dp"), lax.axis_index("vocab")
    x, y = lax.rem(dp, NX), dp // NX
    c, z = lax.rem(vo, NC), vo // NC
    sib = vo + 1 - 2 * c

    def copy(src, dst, send, recv, to_dp, to_vo):
        return pltpu.make_async_remote_copy(
            src_ref=src, dst_ref=dst, send_sem=send, recv_sem=recv, device_id=(to_dp, to_vo), device_id_type=MESH
        )

    def got(ref, recv):
        copy(ref, ref, recv, recv, dp, sib).wait_recv()

    def sent(ref, send):
        copy(ref, ref, send, send, dp, sib).wait_send()

    def each(count, body):
        lax.fori_loop(1, count, lambda k, carry: (body(k), carry)[1], 0)

    def xp(k):
        return lax.rem(x + k, NX)

    def yp(k):
        return lax.rem(y + k + NY, NY)

    def zp(k):
        return lax.rem(z + k, NZ)

    def at_x(k):
        return y * NX + xp(k)

    def at_y(k):
        return yp(k) * NX + x

    def at_z(k):
        return zp(k) * NC + c

    w_copy = pltpu.make_async_copy(head, wv, w_sem)
    w_copy.start()
    gb[...] = jnp.zeros_like(gb)
    wt[:, PADDED - 128:] = jnp.zeros((D, 128), bf16)
    lt[PADDED - 16:, :] = jnp.zeros((16, TOKENS), bf16)
    lab[PADDED - 16:, :] = jnp.zeros((16, TOKENS), bf16)

    barrier = pltpu.get_barrier_semaphore()
    each(LINE, lambda k: pl.semaphore_signal(
        barrier, inc=1, device_id=(dp, lax.rem(vo + k, LINE)), device_id_type=MESH))
    each(PLANE, lambda k: pl.semaphore_signal(
        barrier, inc=1, device_id=(lax.rem(dp + k, PLANE), vo), device_id_type=MESH))
    holder_dp, holder_vo = y * NX + 2 * lax.rem(x, 2) + c, y * NC + x // 2
    taker_dp, taker_core = y * NX + 2 * c + x // 2, lax.rem(x, 2)
    holds = z == y
    own_taker = (taker_dp == dp) & (taker_core == c)

    @pl.when((holder_dp != dp) | (holder_vo != vo))
    def _():
        pl.semaphore_signal(barrier, inc=1, device_id=(holder_dp, holder_vo), device_id_type=MESH)

    takers = jnp.where(holds, NZ - jnp.where(own_taker, 1, 0), 0)
    pl.semaphore_wait(barrier, LINE + PLANE - 2 + takers)

    def transpose_head(first, last):
        def body(b, carry):
            at = pl.multiple_of(b * 256, 256)
            wt[pl.ds(at, 256), 0:ROWS] = wv[:, pl.ds(at, 256)].T
            return carry

        lax.fori_loop(first, last, body, 0)

    def partial_of(rows, i, core):
        start = pl.multiple_of((i * NC + core) * CHUNK, 32)
        product = jnp.dot(wt[pl.ds(start, CHUNK), :], rows[...], preferred_element_type=f32)
        return product.reshape(NX, UNITS, 8, TOKENS)

    def for_sibling(rows, out, arriving, s_sem, r_sem):
        def body(i, carry):
            out[i] = partial_of(rows, i, 1 - c).astype(bf16)
            copy(out.at[i], arriving.at[i], s_sem.at[i], r_sem.at[i], dp, sib).start()
            return carry

        lax.fori_loop(0, NZ, body, 0)

    def own_half(g, rows, arriving, r_sem, by_x, by_z, z_arriving, zs_sem, zr_sem):
        def body(i, carry):
            total = partial_of(rows, i, c)
            got(arriving.at[i], r_sem.at[i])
            total = (total + arriving[i].astype(f32)).astype(bf16)
            for v in range(NX):
                by_x[g, v, i - 4 * g] = total[v, 0:XU]
                by_z[i, v] = total[v, XU:]

            @pl.when(i != z)
            def _():
                copy(by_z.at[i], z_arriving.at[z], zs_sem.at[i], zr_sem.at[z], dp, i * NC + c).start()

            return carry

        lax.fori_loop(4 * g, 4 * g + 4, body, 0)

    def send_x(g, by_x, arriving, s_sem, r_sem):
        for k in (1, 2, 3):
            copy(by_x.at[g, xp(k)], arriving.at[g, x], s_sem.at[g, k], r_sem.at[g, x], at_x(k), vo).start()

    onehot = lax.broadcasted_iota(jnp.int32, (ROWS, TOKENS), 0) == labels[...] - (dp * LINE + vo) * ROWS

    def label_first():
        lab[0:ROWS, :] = onehot.astype(f32).astype(bf16)
        for_sibling(lab, bds, bdr, bc_s, bc_r)

    def label_second():
        for g in range(2):
            own_half(g, lab, bdr, bc_r, bpx, bpz, brz, bzs, bzr)

    @pl.when(c == 0)
    def _():
        hb0[dp] = hidden[:, 0:SHARE]
        for k in (1, 2, 3):
            copy(hb0.at[dp], hb0.at[dp], hs.at[k], hr.at[dp], at_x(k), vo).start()
        w_copy.wait()
        transpose_head(0, 18)
        for k in (1, 2, 3):
            got(hb0.at[at_x(k)], hr.at[at_x(k)])

        def row(k):
            return hb0.at[pl.ds(yp(k) * NX, NX)]

        def row_copy(from_k, to_k, sem):
            return copy(row(from_k), row(from_k), hs.at[sem], hr.at[yp(from_k) * NX], at_y(to_k), vo)

        def across(k):
            copy(row(k), row(k), hds.at[yp(k)], hdr.at[yp(k)], dp, sib).start()

        def row_got(k):
            got(row(k), hr.at[yp(k) * NX])

        row_copy(0, 1, 4).start()
        row_copy(0, -1, 5).start()
        row_copy(0, 4, 6).start()
        across(0)
        label_first()
        row_got(-1)
        row_copy(-1, 1, 7).start()
        row_got(1)
        row_copy(1, -1, 8).start()
        across(-1)
        across(1)
        label_second()
        row_got(4)
        row_copy(4, 1, 9).start()
        row_copy(4, -1, 10).start()
        across(4)
        for k in (2, -2, 3, -3):
            row_got(k)
            across(k)
        for k in (1, 2, 3):
            sent(hb0.at[dp], hs.at[k])
        for sem in range(4, 11):
            sent(row(0), hs.at[sem])

    @pl.when(c == 1)
    def _():
        hb1[dp] = hidden[:, SHARE:]

        def own(k):
            return hb1.at[at_y(k)]

        def spread(k):
            for i in (1, 2, 3):
                copy(own(k), own(k), hs.at[7 + yp(k) * 3 + i], hr.at[at_y(k)], yp(0) * NX + xp(i), vo).start()

        for k in (1, -1, 2, -2, 3, -3, 4):
            copy(own(0), own(0), hs.at[yp(k)], hr.at[dp], at_y(k), vo).start()
        spread(0)
        w_copy.wait()
        transpose_head(0, 18)
        for k in (1, -1):
            got(own(k), hr.at[at_y(k)])
            spread(k)
        label_first()
        for k in (2, -2, 3, -3, 4):
            got(own(k), hr.at[at_y(k)])
            spread(k)
        label_second()

        for k in (0, 1, -1, 2, -2, 3, -3, 4):
            for i in (1, 2, 3):
                slot = yp(k) * NX + xp(i)
                got(hb1.at[slot], hr.at[slot])
            rows = hb1.at[pl.ds(yp(k) * NX, NX)]
            copy(rows, rows, hds.at[yp(k)], hdr.at[yp(k)], dp, sib).start()
        for k in (1, -1, 2, -2, 3, -3, 4):
            sent(own(0), hs.at[yp(k)])
        for k in range(8, 32):
            sent(own(0), hs.at[k])

    for g in range(2):
        send_x(g, bpx, brx, bxs, bxr)
    def across_done(sending, arriving):
        def body(v, carry):
            got(arriving.at[pl.ds(v * NX, NX)], hdr.at[v])
            sent(sending.at[pl.ds(v * NX, NX)], hds.at[v])
            return carry

        lax.fori_loop(0, NY, body, 0)

    pl.when(c == 0)(lambda: across_done(hb0, hb1))
    pl.when(c == 1)(lambda: across_done(hb1, hb0))

    raw = jnp.zeros((ROWS, TOKENS), f32)
    for part, block in enumerate((hb0, hb1, hb1)):
        at = part * SHARE
        skip = max(at - SHARE, 0)
        h2[...] = block[:, :, skip:skip + SHARE].astype(f32).reshape(TOKENS, SHARE).astype(bf16)
        raw += lax.dot_general(
            wv[:, at:at + SHARE], h2[...], (((1,), (1,)), ((), ())), preferred_element_type=f32)
    squash = jnp.tanh(raw * (1.0 / softcap))
    terms = jnp.exp(softcap * squash)

    slope = 1.0 - squash * squash
    den_a[vo] = jnp.concatenate([
        jnp.sum(terms, axis=0, keepdims=True),
        jnp.sum(jnp.where(onehot, terms, 0.0), axis=0, keepdims=True),
        jnp.sum(jnp.where(onehot, slope, 0.0), axis=0, keepdims=True)], axis=1)
    each(LINE, lambda k: copy(
        den_a.at[vo], den_a.at[vo], das.at[k], dar.at[vo], dp, lax.rem(vo + k, LINE)).start())
    lt[0:ROWS, :] = jnp.where(onehot, 0.0, terms * slope).astype(bf16)
    for_sibling(lt, ds_, dr_, c_s, c_r)
    for g in range(2):
        own_half(g, lt, dr_, c_r, px, pz, rz, zs, zr)
        send_x(g, px, rx, xs, xr)
    each(LINE, lambda k: got(den_a.at[vo], dar.at[lax.rem(vo + k, LINE)]))
    each(LINE, lambda k: sent(den_a.at[vo], das.at[k]))
    den_b[dp] = jnp.sum(den_a[...], axis=0)
    each(PLANE, lambda k: copy(
        den_b.at[dp], den_b.at[dp], dbs.at[k], dbr.at[dp], lax.rem(dp + k, PLANE), vo).start())

    each(NZ, lambda k: got(brz.at[0], bzr.at[zp(k)]))
    label_z = bpz[z].astype(f32)
    for k in range(1, NZ):
        label_z += brz[zp(k)].astype(f32)
    bpz[z] = label_z.astype(bf16)
    for g in range(2):
        label_x = bpx[g, x].astype(f32)
        for k in (1, 2, 3):
            got(brx.at[g, 0], bxr.at[g, xp(k)])
            label_x += brx[g, xp(k)].astype(f32)
        bpx[g, x] = label_x.astype(bf16)

    each(PLANE, lambda k: got(den_b.at[dp], dbr.at[lax.rem(dp + k, PLANE)]))
    each(PLANE, lambda k: sent(den_b.at[dp], dbs.at[k]))
    sums = jnp.sum(den_b[...], axis=0)
    inverse = 1.0 / sums[:, 0:TOKENS]
    at_label = ((sums[:, TOKENS:2 * TOKENS] * inverse - 1.0) * sums[:, 2 * TOKENS:]).astype(bf16).astype(f32)

    each(NZ, lambda k: got(rz.at[0], zr.at[zp(k)]))
    total = pz[z].astype(f32)
    for k in range(1, NZ):
        total += rz[zp(k)].astype(f32)
    qz[...] = (total * inverse + bpz[z].astype(f32) * at_label).astype(bf16)
    for k in (1, 2, 3):
        copy(qz.at[xp(k)], r2z.at[x], z2s.at[k], z2r.at[x], at_x(k), vo).start()
    for g in range(2):
        total = px[g, x].astype(f32)
        for k in (1, 2, 3):
            got(rx.at[g, 0], xr.at[g, xp(k)])
            total += rx[g, xp(k)].astype(f32)
        qx[4 * g:4 * g + 4] = (total * inverse + bpx[g, x].astype(f32) * at_label).astype(bf16)
    each(NZ, lambda k: copy(
        qx.at[zp(k)], r2x.at[z], x2s.at[k], x2r.at[z], dp, at_z(k)).start())
    total = qz[x].astype(f32)
    for k in (1, 2, 3):
        got(r2z.at[0], z2r.at[xp(k)])
        total += r2z[xp(k)].astype(f32)
    ry[y, XU:] = total.astype(bf16)
    each(NZ, lambda k: got(r2x.at[0], x2r.at[zp(k)]))
    total = qx[z].astype(f32)
    for k in range(1, NZ):
        total += r2x[zp(k)].astype(f32)
    ry[y, 0:XU] = total.astype(bf16)

    each(NY, lambda k: copy(ry.at[y], ry.at[y], ys.at[k], yr.at[y], at_y(k), vo).start())
    each(NY, lambda k: got(ry.at[0], yr.at[yp(k)]))
    each(NY, lambda k: sent(ry.at[0], ys.at[k]))
    total = ry[0].astype(f32)
    for k in range(1, NY):
        total += ry[k].astype(f32)
    shift = lax.rem(z, 2) * 8 + c * 36

    def quarter(v):
        return gb.at[pl.ds(shift + v * UNITS, UNITS)]

    gb[pl.ds(shift + x * UNITS, UNITS)] = total.astype(bf16)

    @pl.when(holds)
    def _():
        def body(k, carry):
            @pl.when(jnp.logical_not(own_taker) | (k > 0))
            def _():
                copy(quarter(x), rb, bs.at[k], br, taker_dp, zp(k) * NC + taker_core).start()

            return carry

        lax.fori_loop(0, NZ, body, 0)

    for k in (1, 2, 3):
        copy(quarter(x), quarter(x), gs.at[k], gr.at[x], at_x(k), vo).start()
    copy(quarter(x), quarter(x), gds.at[x], gdr.at[x], dp, sib).start()

    @pl.when(holds & own_taker)
    def _():
        rb[...] = gb[pl.ds(shift + x * UNITS, UNITS)]

    for k in (1, 3, 2):
        got(quarter(xp(k)), gr.at[xp(k)])
        copy(quarter(xp(k)), quarter(xp(k)), gds.at[xp(k)], gdr.at[xp(k)], dp, sib).start()

    block = gb[pl.ds(shift, 36)].astype(f32).reshape(CHUNK, TOKENS).astype(bf16)
    token = lax.broadcasted_iota(jnp.int32, (8, TOKENS), 1)
    mine = jnp.where(token == dp * 8 + lax.broadcasted_iota(jnp.int32, (8, TOKENS), 0), 1.0, 0.0).astype(bf16)
    grads[...] = lax.dot_general(
        mine, block, (((1,), (1,)), ((), ())), preferred_element_type=f32).astype(bf16)
    new_factor[...] = decay_rate * factor[...]

    for v in range(NX):
        got(quarter(v), gdr.at[v])

    @pl.when(jnp.logical_not(holds & own_taker))
    def _():
        got(rb, br)

    rows = rb[...].astype(f32).reshape(72, TOKENS).astype(bf16)
    line_row = lax.broadcasted_iota(jnp.int32, (128, 72), 0)
    column = lax.broadcasted_iota(jnp.int32, (128, 72), 1)
    place, within = line_row // 16, lax.rem(line_row, 16)
    pick = jnp.where((within < 9) & (column == place * 9 + within), 1.0, 0.0).astype(bf16)
    spread_rows = jnp.dot(pick, rows, preferred_element_type=f32).astype(bf16)
    columns = gb[...].astype(f32).reshape(640, TOKENS).astype(bf16)
    gram = lax.dot_general(spread_rows, columns, (((1,), (1,)), ((), ())), preferred_element_type=f32)
    tb[...] = gram.reshape(NZ, 16, 640).astype(bf16)

    def to_place(k, carry):
        place = zp(k)

        @pl.when(NZ * c + place != vo)
        def _():
            copy(tb.at[place], rt.at[z], ts.at[place], tr.at[z], dp, NZ * c + place).start()

        return carry

    lax.fori_loop(0, NZ, to_place, 0)
    sender = z // 4

    @pl.when(sender == c)
    def _():
        rt[z] = tb[lax.rem(vo, NZ)]

    scale = (1.0 - decay_rate) * (D / TOKENS)
    for v in range(NZ):
        @pl.when(v * NC + sender != vo)
        def _():
            got(rt.at[0], tr.at[v])

        at = v * NC * CHUNK // 128 * 128
        new_factor[:, at:at + 640] += scale * rt[v].astype(f32)[0:9]

    def places_sent(place, carry):
        @pl.when(NZ * c + place != vo)
        def _():
            sent(tb.at[0], ts.at[place])

        @pl.when(holds & (jnp.logical_not(own_taker) | (place > 0)))
        def _():
            sent(rb, bs.at[place])

        return carry

    lax.fori_loop(0, NZ, places_sent, 0)
    for v in range(NX):
        sent(quarter(v), gds.at[v])
    for k in (1, 2, 3):
        sent(quarter(x), gs.at[k])

    each(NZ, lambda k: sent(pz.at[0], zs.at[zp(k)]))
    each(NZ, lambda k: sent(bpz.at[0], bzs.at[zp(k)]))
    each(NZ, lambda k: sent(qx.at[0], x2s.at[k]))
    for k in (1, 2, 3):
        sent(qz.at[0], z2s.at[k])
        for g in range(2):
            sent(px.at[g, 0], xs.at[g, k])
            sent(bpx.at[g, 0], bxs.at[g, k])
    lax.fori_loop(0, NZ, lambda i, carry: (sent(ds_.at[i], c_s.at[i]), sent(bds.at[i], bc_s.at[i]), carry)[2], 0)


def on_device(hidden, labels, head_weight, factor_rows):
    vmem = pl.BlockSpec(memory_space=pltpu.VMEM)
    dma = pltpu.SemaphoreType.DMA

    def buf(*shape, dtype=bf16):
        return pltpu.VMEM(shape, dtype)

    return pl.pallas_call(
        kernel,
        out_shape=(
            jax.ShapeDtypeStruct(factor_rows.shape, f32),
            jax.ShapeDtypeStruct((TOKENS // PLANE, CHUNK), bf16),
        ),
        in_specs=[vmem, vmem, pl.BlockSpec(memory_space=pl.ANY), vmem],
        out_specs=(vmem, vmem),
        scratch_shapes=[
            buf(ROWS, D), buf(D, PADDED), buf(PLANE, 8, SHARE), buf(PLANE, 8, D - SHARE), buf(TOKENS, SHARE), buf(PADDED, TOKENS),
            buf(NZ, NX, UNITS, 8, TOKENS), buf(NZ, NX, UNITS, 8, TOKENS),
            buf(2, NX, 4, XU, 8, TOKENS), buf(NZ, NX, UNITS - XU, 8, TOKENS),
            buf(2, NX, 4, XU, 8, TOKENS), buf(NZ, NX, UNITS - XU, 8, TOKENS),
            buf(NZ, XU, 8, TOKENS), buf(NX, UNITS - XU, 8, TOKENS),
            buf(NZ, XU, 8, TOKENS), buf(NX, UNITS - XU, 8, TOKENS),
            buf(NY, UNITS, 8, TOKENS), buf(80, 8, TOKENS), buf(UNITS, 8, TOKENS),
            buf(NZ, 16, 640), buf(NZ, 16, 640),
            buf(LINE, 1, 3 * TOKENS, dtype=f32), buf(PLANE, 1, 3 * TOKENS, dtype=f32), buf(PADDED, TOKENS),
            buf(NZ, NX, UNITS, 8, TOKENS), buf(NZ, NX, UNITS, 8, TOKENS),
            buf(2, NX, 4, XU, 8, TOKENS), buf(NZ, NX, UNITS - XU, 8, TOKENS),
            buf(2, NX, 4, XU, 8, TOKENS), buf(NZ, NX, UNITS - XU, 8, TOKENS),
            dma, dma((32,)), dma((32,)), dma((8,)), dma((8,)),
            dma((LINE,)), dma((LINE,)), dma((PLANE,)), dma((PLANE,)), dma((NZ,)), dma((NZ,)),
            dma((2, NX)), dma((2, NX)), dma((NZ,)), dma((NZ,)), dma((NZ,)), dma((NZ,)), dma((NX,)), dma((NX,)),
            dma((NY,)), dma((NY,)), dma((NX,)), dma((NX,)), dma((NZ,)), dma, dma((NZ,)), dma((NZ,)), dma((NX,)), dma((NX,)),
            dma((NZ,)), dma((NZ,)), dma((2, NX)), dma((2, NX)), dma((NZ,)), dma((NZ,)),
        ],
        compiler_params=pltpu.CompilerParams(
            collective_id=0, has_side_effects=True, vmem_limit_bytes=56 * 2**20),
        cost_estimate=pl.CostEstimate(flops=4 * 500 * 256 * 4608, bytes_accessed=6 * 2**20, transcendentals=2 * 500 * 256),
    )(hidden, labels.reshape(1, TOKENS), head_weight, factor_rows)


def solution(mesh):
    placed = (P("dp", None), P(), P(("dp", "vocab"), None), P(("dp", "vocab"), None))
    return jax.shard_map(
        on_device,
        mesh=mesh,
        in_specs=placed,
        out_specs=(P(("dp", "vocab"), None), P("dp", "vocab")),
        check_vma=False,
    )
```

time: 109 us -> 88.4 us (0.81); the launches traced: 109 us -> 87.1 us
  Pallas kernels: 106 us -> 83.5 us
    pallas_call x1, Pallas kernels: 106 us -> 83.5 us  [on_device(): pl.pallas_call(kernel, out_shape=(jax.ShapeDtypeStruct(factor_rows.shape,...]
where the time goes in v2:
time: 88.4 us; the launch traced here: 87.1 us
  Pallas kernels  83.5 us (94%)
  local copies, waits for them, and re-layouts  2.98 us (3%)
    pallas_call x1, Pallas kernels, on_device(): pl.pallas_call(kernel, out_shape=(jax.ShapeDtypeStruct(factor_rows.shape,...  83.5 us
    unnamed x2, local copies, waits for them, and re-layouts  2.98 us

profile of v2, /device:TPU:1, one launch (start us, length us, event | category | flops | bytes accessed | tf_op | source)
XLA Modules:
  0.0 87.1 jit_solution(7811578657835339797)
XLA Ops:
  0.6 83.5 %shard_map.59 = (f32[9,4608]{1,0:T(8,128)}, bf16[8,288]{1,0:T(8,128)(2,1)}) custom-call(bf16[8,4608]{1,0:T(8,128)(2,1)} %hidden.1, s32[1,256]{1,0:T(1,128)} %bitcast.1, bf16[500,4608]{1,0:T(8,128)(2,1)} %head.1, f32[9,4608]{1,0:T(8,128)} %factor.1), custom_call_target="tpu_custom_call" | custom-call | flops 2359296000 | bytes 6291456 | tf_op jit(solution)/shard_map/pallas_call | solution.py:429
  84.2 1.7 %copy.8 = f32[9,4608]{1,0:T(8,128)} copy(f32[9,4608]{1,0:T(8,128)} %get-tuple-element.4) | data formatting | bytes 331776
  85.9 1.3 %copy.9 = bf16[8,288]{1,0:T(8,128)(2,1)} copy(bf16[8,288]{1,0:T(8,128)(2,1)} %get-tuple-element.5) | data formatting | bytes 9216

commit v3 on v2

--- a/solution.py
+++ b/solution.py
@@ -21,9 +21,9 @@
 
 
 def kernel(
-    hidden, labels, head, factor, new_factor, grads,
-    wv, wt, hb0, hb1, h2, lt, ds_, dr_, px, pz, rx, rz, qx, qz, r2x, r2z, ry, gb, rb, tb, rt, den_a, den_b, lab, bds, bdr, bpx, bpz, brx, brz,
-    w_sem, hs, hr, hds, hdr, das, dar, dbs, dbr, c_s, c_r, xs, xr, zs, zr, x2s, x2r, z2s, z2r,
+    hidden_in, labels_in, head, gram_rows, grads,
+    hidden, labels, wv, wt, hb0, hb1, h2, lt, ds_, dr_, px, pz, rx, rz, qx, qz, r2x, r2z, ry, gb, rb, tb, rt, den_a, den_b, lab, bds, bdr, bpx, bpz, brx, brz,
+    w_sem, in_sem, hs, hr, hds, hdr, das, dar, dbs, dbr, c_s, c_r, xs, xr, zs, zr, x2s, x2r, z2s, z2r,
     ys, yr, gs, gr, bs, br, ts, tr, gds, gdr, bc_s, bc_r, bxs, bxr, bzs, bzr,
 ):
     dp, vo = lax.axis_index("dp"), lax.axis_index("vocab")
@@ -64,28 +64,24 @@
         return zp(k) * NC + c
 
     w_copy = pltpu.make_async_copy(head, wv, w_sem)
+    hidden_copy = pltpu.make_async_copy(hidden_in, hidden, in_sem.at[0])
+    labels_copy = pltpu.make_async_copy(labels_in, labels, in_sem.at[1])
+    hidden_copy.start()
+    labels_copy.start()
     w_copy.start()
     gb[...] = jnp.zeros_like(gb)
-    wt[:, PADDED - 128:] = jnp.zeros((D, 128), bf16)
-    lt[PADDED - 16:, :] = jnp.zeros((16, TOKENS), bf16)
-    lab[PADDED - 16:, :] = jnp.zeros((16, TOKENS), bf16)
 
     barrier = pltpu.get_barrier_semaphore()
     each(LINE, lambda k: pl.semaphore_signal(
         barrier, inc=1, device_id=(dp, lax.rem(vo + k, LINE)), device_id_type=MESH))
     each(PLANE, lambda k: pl.semaphore_signal(
         barrier, inc=1, device_id=(lax.rem(dp + k, PLANE), vo), device_id_type=MESH))
-    holder_dp, holder_vo = y * NX + 2 * lax.rem(x, 2) + c, y * NC + x // 2
-    taker_dp, taker_core = y * NX + 2 * c + x // 2, lax.rem(x, 2)
-    holds = z == y
-    own_taker = (taker_dp == dp) & (taker_core == c)
-
-    @pl.when((holder_dp != dp) | (holder_vo != vo))
-    def _():
-        pl.semaphore_signal(barrier, inc=1, device_id=(holder_dp, holder_vo), device_id_type=MESH)
-
-    takers = jnp.where(holds, NZ - jnp.where(own_taker, 1, 0), 0)
-    pl.semaphore_wait(barrier, LINE + PLANE - 2 + takers)
+    wt[:, PADDED - 128:] = jnp.zeros((D, 128), bf16)
+    lt[PADDED - 16:, :] = jnp.zeros((16, TOKENS), bf16)
+    lab[PADDED - 16:, :] = jnp.zeros((16, TOKENS), bf16)
+    pl.semaphore_wait(barrier, LINE + PLANE - 2)
+    hidden_copy.wait()
+    labels_copy.wait()
 
     def transpose_head(first, last):
         def body(b, carry):
@@ -312,6 +308,9 @@
     total = ry[0].astype(f32)
     for k in range(1, NY):
         total += ry[k].astype(f32)
+    taker_dp, taker_core = y * NX + 2 * c + x // 2, lax.rem(x, 2)
+    holds = z == y
+    own_taker = (taker_dp == dp) & (taker_core == c)
     shift = lax.rem(z, 2) * 8 + c * 36
 
     def quarter(v):
@@ -347,7 +346,7 @@
     mine = jnp.where(token == dp * 8 + lax.broadcasted_iota(jnp.int32, (8, TOKENS), 0), 1.0, 0.0).astype(bf16)
     grads[...] = lax.dot_general(
         mine, block, (((1,), (1,)), ((), ())), preferred_element_type=f32).astype(bf16)
-    new_factor[...] = decay_rate * factor[...]
+    gram_rows[...] = jnp.zeros_like(gram_rows)
 
     for v in range(NX):
         got(quarter(v), gdr.at[v])
@@ -382,14 +381,13 @@
     def _():
         rt[z] = tb[lax.rem(vo, NZ)]
 
-    scale = (1.0 - decay_rate) * (D / TOKENS)
     for v in range(NZ):
         @pl.when(v * NC + sender != vo)
         def _():
             got(rt.at[0], tr.at[v])
 
         at = v * NC * CHUNK // 128 * 128
-        new_factor[:, at:at + 640] += scale * rt[v].astype(f32)[0:9]
+        gram_rows[:, at:at + 640] += rt[v].astype(f32)[0:9]
 
     def places_sent(place, carry):
         @pl.when(NZ * c + place != vo)
@@ -419,6 +417,12 @@
     lax.fori_loop(0, NZ, lambda i, carry: (sent(ds_.at[i], c_s.at[i]), sent(bds.at[i], bc_s.at[i]), carry)[2], 0)
 
 
+def update(gram_rows, grads_in, factor, new_factor, grads):
+    scale = (1.0 - decay_rate) * (D / TOKENS)
+    new_factor[...] = decay_rate * factor[...] + scale * gram_rows[...]
+    grads[...] = grads_in[...]
+
+
 def on_device(hidden, labels, head_weight, factor_rows):
     vmem = pl.BlockSpec(memory_space=pltpu.VMEM)
     dma = pltpu.SemaphoreType.DMA
@@ -426,16 +430,17 @@
     def buf(*shape, dtype=bf16):
         return pltpu.VMEM(shape, dtype)
 
-    return pl.pallas_call(
+    any_space = pl.BlockSpec(memory_space=pl.ANY)
+    gram_rows, grads = pl.pallas_call(
         kernel,
         out_shape=(
             jax.ShapeDtypeStruct(factor_rows.shape, f32),
             jax.ShapeDtypeStruct((TOKENS // PLANE, CHUNK), bf16),
         ),
-        in_specs=[vmem, vmem, pl.BlockSpec(memory_space=pl.ANY), vmem],
+        in_specs=[any_space] * 3,
         out_specs=(vmem, vmem),
         scratch_shapes=[
-            buf(ROWS, D), buf(D, PADDED), buf(PLANE, 8, SHARE), buf(PLANE, 8, D - SHARE), buf(TOKENS, SHARE), buf(PADDED, TOKENS),
+            buf(TOKENS // PLANE, D), buf(1, TOKENS, dtype=jnp.int32), buf(ROWS, D), buf(D, PADDED), buf(PLANE, 8, SHARE), buf(PLANE, 8, D - SHARE), buf(TOKENS, SHARE), buf(PADDED, TOKENS),
             buf(NZ, NX, UNITS, 8, TOKENS), buf(NZ, NX, UNITS, 8, TOKENS),
             buf(2, NX, 4, XU, 8, TOKENS), buf(NZ, NX, UNITS - XU, 8, TOKENS),
             buf(2, NX, 4, XU, 8, TOKENS), buf(NZ, NX, UNITS - XU, 8, TOKENS),
@@ -447,7 +452,7 @@
             buf(NZ, NX, UNITS, 8, TOKENS), buf(NZ, NX, UNITS, 8, TOKENS),
             buf(2, NX, 4, XU, 8, TOKENS), buf(NZ, NX, UNITS - XU, 8, TOKENS),
             buf(2, NX, 4, XU, 8, TOKENS), buf(NZ, NX, UNITS - XU, 8, TOKENS),
-            dma, dma((32,)), dma((32,)), dma((8,)), dma((8,)),
+            dma, dma((2,)), dma((32,)), dma((32,)), dma((8,)), dma((8,)),
             dma((LINE,)), dma((LINE,)), dma((PLANE,)), dma((PLANE,)), dma((NZ,)), dma((NZ,)),
             dma((2, NX)), dma((2, NX)), dma((NZ,)), dma((NZ,)), dma((NZ,)), dma((NZ,)), dma((NX,)), dma((NX,)),
             dma((NY,)), dma((NY,)), dma((NX,)), dma((NX,)), dma((NZ,)), dma, dma((NZ,)), dma((NZ,)), dma((NX,)), dma((NX,)),
@@ -456,7 +461,16 @@
         compiler_params=pltpu.CompilerParams(
             collective_id=0, has_side_effects=True, vmem_limit_bytes=56 * 2**20),
         cost_estimate=pl.CostEstimate(flops=4 * 500 * 256 * 4608, bytes_accessed=6 * 2**20, transcendentals=2 * 500 * 256),
-    )(hidden, labels.reshape(1, TOKENS), head_weight, factor_rows)
+    )(hidden, labels.reshape(1, TOKENS), head_weight)
+    return pl.pallas_call(
+        update,
+        out_shape=(
+            jax.ShapeDtypeStruct(factor_rows.shape, f32),
+            jax.ShapeDtypeStruct(grads.shape, bf16),
+        ),
+        in_specs=[vmem] * 3,
+        out_specs=(vmem, vmem),
+    )(gram_rows, grads, factor_rows)
 
 
 def solution(mesh):

time: 88.4 us -> 87.4 us (0.989); the launches traced: 87.1 us -> 87.3 us
  Pallas kernels: 83.5 us -> 86.6 us
  local copies, waits for them, and re-layouts: 2.98 us -> 0 us
    unnamed x2 -> x0, local copies, waits for them, and re-layouts: 2.98 us -> none
    pallas_call x0 -> x1, Pallas kernels: none -> 1.84 us  [on_device(): pl.pallas_call(update, out_shape=(jax.ShapeDtypeStruct(factor_rows.shape,...]
    pallas_call x1, Pallas kernels: 83.5 us -> 84.8 us  [on_device(): pl.pallas_call(kernel, out_shape=(jax.ShapeDtypeStruct(factor_rows.shape,...]
where the time goes in v3:
time: 87.4 us; the launch traced here: 87.3 us
  Pallas kernels  86.6 us (99%)
    pallas_call x1, Pallas kernels, on_device(): pl.pallas_call(kernel, out_shape=(jax.ShapeDtypeStruct(factor_rows.shape,...  84.8 us
    pallas_call x1, Pallas kernels, on_device(): pl.pallas_call(update, out_shape=(jax.ShapeDtypeStruct(factor_rows.shape,...  1.84 us

profile of v3, /device:TPU:1, one launch (start us, length us, event | category | flops | bytes accessed | tf_op | source)
XLA Modules:
  0.0 87.3 jit_solution(15121691175707407849)
XLA Ops:
  0.6 84.8 %shard_map.59 = (f32[9,4608]{1,0:T(8,128)}, bf16[8,288]{1,0:T(8,128)(2,1)}) custom-call(bf16[8,4608]{1,0:T(8,128)(2,1)} %hidden_in.1, s32[1,256]{1,0:T(1,128)} %bitcast.1, bf16[500,4608]{1,0:T(8,128)(2,1)} %head.1), custom_call_target="tpu_custom_call" | custom-call | flops 2359296000 | bytes 6291456 | tf_op jit(solution)/shard_map/pallas_call | solution.py:434
  85.4 1.8 %shard_map.60 = (f32[9,4608]{1,0:T(8,128)}, bf16[8,288]{1,0:T(8,128)(2,1)}) custom-call(f32[9,4608]{1,0:T(8,128)} %get-tuple-element.4.gram_rows, bf16[8,288]{1,0:T(8,128)(2,1)} %get-tuple-element.5.grads_in, f32[9,4608]{1,0:T(8,128)} %factor.1), custom_call_target="tpu_custom_call" | custom-call | tf_op jit(solution)/shard_map/pallas_call | solution.py:465

commit v4 on v3

--- a/solution.py
+++ b/solution.py
@@ -12,10 +12,11 @@
 PLANE, LINE = NX * NY, NZ * NC
 D, TOKENS, ROWS = 4608, 256, 500
 PADDED = 512
-SHARE = D // 3
+SHARE = D // 4
 CHUNK = D // LINE
 UNITS = CHUNK // 8 // NX
-XU = 6
+XU, ZU, YU = 5, 2, 2
+LXU, LZU = 2, 5
 MESH = pl.DeviceIdType.MESH
 f32, bf16 = jnp.float32, jnp.bfloat16
 
@@ -23,8 +24,11 @@
 def kernel(
     hidden_in, labels_in, head, gram_rows, grads,
     hidden, labels, wv, wt, hb0, hb1, h2, lt, ds_, dr_, px, pz, rx, rz, qx, qz, r2x, r2z, ry, gb, rb, tb, rt, den_a, den_b, lab, bds, bdr, bpx, bpz, brx, brz,
+    py, r1y, bpy, br1y, qy, r2y, sy, r3y, yb,
+    bqx, bqz, bqy, br2x, br2z, br2y, label,
     w_sem, in_sem, hs, hr, hds, hdr, das, dar, dbs, dbr, c_s, c_r, xs, xr, zs, zr, x2s, x2r, z2s, z2r,
     ys, yr, gs, gr, bs, br, ts, tr, gds, gdr, bc_s, bc_r, bxs, bxr, bzs, bzr,
+    y1s, y1r, by1s, by1r, y2s, y2r, y3s, y3r, y4s, y4r, bx2s, bx2r, bz2s, bz2r, by2s, by2r,
 ):
     dp, vo = lax.axis_index("dp"), lax.axis_index("vocab")
     x, y = lax.rem(dp, NX), dp // NX
@@ -104,19 +108,24 @@
 
         lax.fori_loop(0, NZ, body, 0)
 
-    def own_half(g, rows, arriving, r_sem, by_x, by_z, z_arriving, zs_sem, zr_sem):
+    def own_half(g, rows, arriving, r_sem, by_x, by_z, z_arriving, zs_sem, zr_sem, by_y, y_arriving, ys_sem, yr_sem):
         def body(i, carry):
             total = partial_of(rows, i, c)
             got(arriving.at[i], r_sem.at[i])
             total = (total + arriving[i].astype(f32)).astype(bf16)
             for v in range(NX):
-                by_x[g, v, i - 4 * g] = total[v, 0:XU]
-                by_z[i, v] = total[v, XU:]
+                by_x[g, v, i - 4 * g] = total[v, 0:by_x.shape[3]]
+                by_z[i, v] = total[v, by_x.shape[3]:XU + ZU]
+                by_y[i, v] = total[v, XU + ZU:]
 
             @pl.when(i != z)
             def _():
                 copy(by_z.at[i], z_arriving.at[z], zs_sem.at[i], zr_sem.at[z], dp, i * NC + c).start()
 
+            @pl.when(i != y)
+            def _():
+                copy(by_y.at[i], y_arriving.at[y], ys_sem.at[i], yr_sem.at[y], i * NX + x, vo).start()
+
             return carry
 
         lax.fori_loop(4 * g, 4 * g + 4, body, 0)
@@ -133,7 +142,7 @@
 
     def label_second():
         for g in range(2):
-            own_half(g, lab, bdr, bc_r, bpx, bpz, brz, bzs, bzr)
+            own_half(g, lab, bdr, bc_r, bpx, bpz, brz, bzs, bzr, bpy, br1y, by1s, by1r)
 
     @pl.when(c == 0)
     def _():
@@ -231,7 +240,7 @@
     pl.when(c == 1)(lambda: across_done(hb1, hb0))
 
     raw = jnp.zeros((ROWS, TOKENS), f32)
-    for part, block in enumerate((hb0, hb1, hb1)):
+    for part, block in enumerate((hb0, hb1, hb1, hb1)):
         at = part * SHARE
         skip = max(at - SHARE, 0)
         h2[...] = block[:, :, skip:skip + SHARE].astype(f32).reshape(TOKENS, SHARE).astype(bf16)
@@ -250,7 +259,7 @@
     lt[0:ROWS, :] = jnp.where(onehot, 0.0, terms * slope).astype(bf16)
     for_sibling(lt, ds_, dr_, c_s, c_r)
     for g in range(2):
-        own_half(g, lt, dr_, c_r, px, pz, rz, zs, zr)
+        own_half(g, lt, dr_, c_r, px, pz, rz, zs, zr, py, r1y, y1s, y1r)
         send_x(g, px, rx, xs, xr)
     each(LINE, lambda k: got(den_a.at[vo], dar.at[lax.rem(vo + k, LINE)]))
     each(LINE, lambda k: sent(den_a.at[vo], das.at[k]))
@@ -258,17 +267,50 @@
     each(PLANE, lambda k: copy(
         den_b.at[dp], den_b.at[dp], dbs.at[k], dbr.at[dp], lax.rem(dp + k, PLANE), vo).start())
 
-    each(NZ, lambda k: got(brz.at[0], bzr.at[zp(k)]))
-    label_z = bpz[z].astype(f32)
-    for k in range(1, NZ):
-        label_z += brz[zp(k)].astype(f32)
-    bpz[z] = label_z.astype(bf16)
-    for g in range(2):
-        label_x = bpx[g, x].astype(f32)
+    def summed(own, arriving, count, at, recv):
+        total = own.astype(f32)
+        for k in range(1, count):
+            got(arriving.at[0], recv.at[at(k)])
+            total += arriving[at(k)].astype(f32)
+        return total
+
+    def x_sum(g, own, arriving, recv):
+        total = own[g, x].astype(f32)
         for k in (1, 2, 3):
-            got(brx.at[g, 0], bxr.at[g, xp(k)])
-            label_x += brx[g, xp(k)].astype(f32)
-        bpx[g, x] = label_x.astype(bf16)
+            got(arriving.at[g, 0], recv.at[g, xp(k)])
+            total += arriving[g, xp(k)].astype(f32)
+        return total.astype(bf16)
+
+    def over_x(rows, arriving, s_sem, r_sem):
+        for k in (1, 2, 3):
+            copy(rows.at[xp(k)], arriving.at[x], s_sem.at[k], r_sem.at[x], at_x(k), vo).start()
+
+    def over_z(g, rows, arriving, s_sem, r_sem):
+        def body(i, carry):
+            @pl.when(i != z)
+            def _():
+                copy(rows.at[i], arriving.at[z], s_sem.at[i], r_sem.at[z], dp, i * NC + c).start()
+
+            return carry
+
+        lax.fori_loop(4 * g, 4 * g + 4, body, 0)
+
+    def second_step(by_x, by_z, by_y, rx_, rz_, ry_, xr_, zr_, yr_, qx_, qz_, qy_, r2x_, r2z_, r2y_,
+                    x2s_, x2r_, z2s_, z2r_, y2s_, y2r_):
+        qy_[...] = summed(by_y[y], ry_, NY, yp, yr_).astype(bf16)
+        over_x(qy_, r2y_, y2s_, y2r_)
+        qz_[...] = summed(by_z[z], rz_, NZ, zp, zr_).astype(bf16)
+        over_x(qz_, r2z_, z2s_, z2r_)
+        for g in range(2):
+            qx_[4 * g:4 * g + 4] = x_sum(g, by_x, rx_, xr_)
+            over_z(g, qx_, r2x_, x2s_, x2r_)
+
+    second_step(bpx, bpz, bpy, brx, brz, br1y, bxr, bzr, by1r, bqx, bqz, bqy, br2x, br2z, br2y,
+                bx2s, bx2r, bz2s, bz2r, by2s, by2r)
+    second_step(px, pz, py, rx, rz, r1y, xr, zr, y1r, qx, qz, qy, r2x, r2z, r2y, x2s, x2r, z2s, z2r, y2s, y2r)
+    label[XU + ZU:] = summed(bqy[x], br2y, NX, xp, by2r).astype(bf16)
+    label[LXU:XU + ZU] = summed(bqz[x], br2z, NX, xp, bz2r).astype(bf16)
+    label[0:LXU] = summed(bqx[z], br2x, NZ, zp, bx2r).astype(bf16)
 
     each(PLANE, lambda k: got(den_b.at[dp], dbr.at[lax.rem(dp + k, PLANE)]))
     each(PLANE, lambda k: sent(den_b.at[dp], dbs.at[k]))
@@ -276,33 +318,29 @@
     inverse = 1.0 / sums[:, 0:TOKENS]
     at_label = ((sums[:, TOKENS:2 * TOKENS] * inverse - 1.0) * sums[:, 2 * TOKENS:]).astype(bf16).astype(f32)
 
-    each(NZ, lambda k: got(rz.at[0], zr.at[zp(k)]))
-    total = pz[z].astype(f32)
-    for k in range(1, NZ):
-        total += rz[zp(k)].astype(f32)
-    qz[...] = (total * inverse + bpz[z].astype(f32) * at_label).astype(bf16)
-    for k in (1, 2, 3):
-        copy(qz.at[xp(k)], r2z.at[x], z2s.at[k], z2r.at[x], at_x(k), vo).start()
-    for g in range(2):
-        total = px[g, x].astype(f32)
-        for k in (1, 2, 3):
-            got(rx.at[g, 0], xr.at[g, xp(k)])
-            total += rx[g, xp(k)].astype(f32)
-        qx[4 * g:4 * g + 4] = (total * inverse + bpx[g, x].astype(f32) * at_label).astype(bf16)
-    each(NZ, lambda k: copy(
-        qx.at[zp(k)], r2x.at[z], x2s.at[k], x2r.at[z], dp, at_z(k)).start())
-    total = qz[x].astype(f32)
-    for k in (1, 2, 3):
-        got(r2z.at[0], z2r.at[xp(k)])
-        total += r2z[xp(k)].astype(f32)
-    ry[y, XU:] = total.astype(bf16)
-    each(NZ, lambda k: got(r2x.at[0], x2r.at[zp(k)]))
-    total = qx[z].astype(f32)
-    for k in range(1, NZ):
-        total += r2x[zp(k)].astype(f32)
-    ry[y, 0:XU] = total.astype(bf16)
+    def joined(total, first, last):
+        return (total * inverse + label[first:last].astype(f32) * at_label).astype(bf16)
+
+    sy[...] = joined(summed(qy[x], r2y, NX, xp, y2r), XU + ZU, UNITS)
+
+    @pl.when(z != y)
+    def _():
+        copy(sy, r3y.at[z], y3s, y3r.at[z], dp, y * NC + c).start()
+
+    ry[y, XU:] = joined(summed(qz[x], r2z, NX, xp, z2r), XU, XU + ZU)
+    ry[y, 0:XU] = joined(summed(qx[z], r2x, NZ, zp, x2r), 0, XU)
 
     each(NY, lambda k: copy(ry.at[y], ry.at[y], ys.at[k], yr.at[y], at_y(k), vo).start())
+
+    @pl.when(z == y)
+    def _():
+        each(NZ, lambda k: got(r3y.at[0], y3r.at[zp(k)]))
+        done = sy[...].astype(f32)
+        for k in range(1, NZ):
+            done += r3y[zp(k)].astype(f32)
+        yb[...] = done.astype(bf16)
+        each(NY, lambda k: copy(yb, yb, y4s.at[k], y4r, at_y(k), vo).start())
+
     each(NY, lambda k: got(ry.at[0], yr.at[yp(k)]))
     each(NY, lambda k: sent(ry.at[0], ys.at[k]))
     total = ry[0].astype(f32)
@@ -316,7 +354,12 @@
     def quarter(v):
         return gb.at[pl.ds(shift + v * UNITS, UNITS)]
 
-    gb[pl.ds(shift + x * UNITS, UNITS)] = total.astype(bf16)
+    @pl.when(z != y)
+    def _():
+        got(yb, y4r)
+
+    gb[pl.ds(shift + x * UNITS, XU + ZU)] = total.astype(bf16)
+    gb[pl.ds(shift + x * UNITS + XU + ZU, YU)] = yb[...]
 
     @pl.when(holds)
     def _():
@@ -406,11 +449,25 @@
     for k in (1, 2, 3):
         sent(quarter(x), gs.at[k])
 
+    @pl.when(z == y)
+    def _():
+        each(NY, lambda k: sent(yb, y4s.at[k]))
+
+    @pl.when(z != y)
+    def _():
+        sent(sy, y3s)
+
+    each(NY, lambda k: sent(py.at[0], y1s.at[yp(k)]))
+    each(NY, lambda k: sent(bpy.at[0], by1s.at[yp(k)]))
     each(NZ, lambda k: sent(pz.at[0], zs.at[zp(k)]))
     each(NZ, lambda k: sent(bpz.at[0], bzs.at[zp(k)]))
-    each(NZ, lambda k: sent(qx.at[0], x2s.at[k]))
+    each(NZ, lambda k: sent(qx.at[0], x2s.at[zp(k)]))
+    each(NZ, lambda k: sent(bqx.at[0], bx2s.at[zp(k)]))
     for k in (1, 2, 3):
         sent(qz.at[0], z2s.at[k])
+        sent(qy.at[0], y2s.at[k])
+        sent(bqz.at[0], bz2s.at[k])
+        sent(bqy.at[0], by2s.at[k])
         for g in range(2):
             sent(px.at[g, 0], xs.at[g, k])
             sent(bpx.at[g, 0], bxs.at[g, k])
@@ -442,21 +499,28 @@
         scratch_shapes=[
             buf(TOKENS // PLANE, D), buf(1, TOKENS, dtype=jnp.int32), buf(ROWS, D), buf(D, PADDED), buf(PLANE, 8, SHARE), buf(PLANE, 8, D - SHARE), buf(TOKENS, SHARE), buf(PADDED, TOKENS),
             buf(NZ, NX, UNITS, 8, TOKENS), buf(NZ, NX, UNITS, 8, TOKENS),
-            buf(2, NX, 4, XU, 8, TOKENS), buf(NZ, NX, UNITS - XU, 8, TOKENS),
-            buf(2, NX, 4, XU, 8, TOKENS), buf(NZ, NX, UNITS - XU, 8, TOKENS),
-            buf(NZ, XU, 8, TOKENS), buf(NX, UNITS - XU, 8, TOKENS),
-            buf(NZ, XU, 8, TOKENS), buf(NX, UNITS - XU, 8, TOKENS),
-            buf(NY, UNITS, 8, TOKENS), buf(80, 8, TOKENS), buf(UNITS, 8, TOKENS),
+            buf(2, NX, 4, XU, 8, TOKENS), buf(NZ, NX, ZU, 8, TOKENS),
+            buf(2, NX, 4, XU, 8, TOKENS), buf(NZ, NX, ZU, 8, TOKENS),
+            buf(NZ, XU, 8, TOKENS), buf(NX, ZU, 8, TOKENS),
+            buf(NZ, XU, 8, TOKENS), buf(NX, ZU, 8, TOKENS),
+            buf(NY, XU + ZU, 8, TOKENS), buf(80, 8, TOKENS), buf(UNITS, 8, TOKENS),
             buf(NZ, 16, 640), buf(NZ, 16, 640),
             buf(LINE, 1, 3 * TOKENS, dtype=f32), buf(PLANE, 1, 3 * TOKENS, dtype=f32), buf(PADDED, TOKENS),
             buf(NZ, NX, UNITS, 8, TOKENS), buf(NZ, NX, UNITS, 8, TOKENS),
-            buf(2, NX, 4, XU, 8, TOKENS), buf(NZ, NX, UNITS - XU, 8, TOKENS),
-            buf(2, NX, 4, XU, 8, TOKENS), buf(NZ, NX, UNITS - XU, 8, TOKENS),
+            buf(2, NX, 4, LXU, 8, TOKENS), buf(NZ, NX, LZU, 8, TOKENS),
+            buf(2, NX, 4, LXU, 8, TOKENS), buf(NZ, NX, LZU, 8, TOKENS),
+            buf(NY, NX, YU, 8, TOKENS), buf(NY, NX, YU, 8, TOKENS), buf(NY, NX, YU, 8, TOKENS), buf(NY, NX, YU, 8, TOKENS),
+            buf(NX, YU, 8, TOKENS), buf(NX, YU, 8, TOKENS), buf(YU, 8, TOKENS), buf(NZ, YU, 8, TOKENS),
+            buf(YU, 8, TOKENS),
+            buf(NZ, LXU, 8, TOKENS), buf(NX, LZU, 8, TOKENS), buf(NX, YU, 8, TOKENS),
+            buf(NZ, LXU, 8, TOKENS), buf(NX, LZU, 8, TOKENS), buf(NX, YU, 8, TOKENS), buf(UNITS, 8, TOKENS),
             dma, dma((2,)), dma((32,)), dma((32,)), dma((8,)), dma((8,)),
             dma((LINE,)), dma((LINE,)), dma((PLANE,)), dma((PLANE,)), dma((NZ,)), dma((NZ,)),
             dma((2, NX)), dma((2, NX)), dma((NZ,)), dma((NZ,)), dma((NZ,)), dma((NZ,)), dma((NX,)), dma((NX,)),
             dma((NY,)), dma((NY,)), dma((NX,)), dma((NX,)), dma((NZ,)), dma, dma((NZ,)), dma((NZ,)), dma((NX,)), dma((NX,)),
             dma((NZ,)), dma((NZ,)), dma((2, NX)), dma((2, NX)), dma((NZ,)), dma((NZ,)),
+            dma((NY,)), dma((NY,)), dma((NY,)), dma((NY,)), dma((NX,)), dma((NX,)), dma, dma((NZ,)), dma((NY,)), dma,
+            dma((NZ,)), dma((NZ,)), dma((NX,)), dma((NX,)), dma((NX,)), dma((NX,)),
         ],
         compiler_params=pltpu.CompilerParams(
             collective_id=0, has_side_effects=True, vmem_limit_bytes=56 * 2**20),

time: 87.4 us -> 83.7 us (0.958); the launches traced: 87.3 us -> 82 us
  Pallas kernels: 86.6 us -> 81.4 us
    pallas_call x1, Pallas kernels: 84.8 us -> 79.5 us  [on_device(): pl.pallas_call(kernel, out_shape=(jax.ShapeDtypeStruct(factor_rows.shape,...]
where the time goes in v4:
time: 83.7 us; the launch traced here: 82 us
  Pallas kernels  81.4 us (97%)
    pallas_call x1, Pallas kernels, on_device(): pl.pallas_call(kernel, out_shape=(jax.ShapeDtypeStruct(factor_rows.shape,...  79.5 us
    pallas_call x1, Pallas kernels, on_device(): pl.pallas_call(update, out_shape=(jax.ShapeDtypeStruct(factor_rows.shape,...  1.84 us

profile of v4, /device:TPU:1, one launch (start us, length us, event | category | flops | bytes accessed | tf_op | source)
XLA Modules:
  0.0 82.0 jit_solution(625486372824490434)
XLA Ops:
  0.6 79.5 %shard_map.59 = (f32[9,4608]{1,0:T(8,128)}, bf16[8,288]{1,0:T(8,128)(2,1)}) custom-call(bf16[8,4608]{1,0:T(8,128)(2,1)} %hidden_in.1, s32[1,256]{1,0:T(1,128)} %bitcast.1, bf16[500,4608]{1,0:T(8,128)(2,1)} %head.1), custom_call_target="tpu_custom_call" | custom-call | flops 2359296000 | bytes 6291456 | tf_op jit(solution)/shard_map/pallas_call | solution.py:491
  80.2 1.8 %shard_map.60 = (f32[9,4608]{1,0:T(8,128)}, bf16[8,288]{1,0:T(8,128)(2,1)}) custom-call(f32[9,4608]{1,0:T(8,128)} %get-tuple-element.4.gram_rows, bf16[8,288]{1,0:T(8,128)(2,1)} %get-tuple-element.5.grads_in, f32[9,4608]{1,0:T(8,128)} %factor.1), custom_call_target="tpu_custom_call" | custom-call | tf_op jit(solution)/shard_map/pallas_call | solution.py:529

commit v5 on v4

--- a/solution.py
+++ b/solution.py
@@ -103,7 +103,7 @@
     def for_sibling(rows, out, arriving, s_sem, r_sem):
         def body(i, carry):
             out[i] = partial_of(rows, i, 1 - c).astype(bf16)
-            copy(out.at[i], arriving.at[i], s_sem.at[i], r_sem.at[i], dp, sib).start()
+            copy(out.at[i], arriving.at[i], s_sem, r_sem.at[i], dp, sib).start()
             return carry
 
         lax.fori_loop(0, NZ, body, 0)
@@ -120,11 +120,11 @@
 
             @pl.when(i != z)
             def _():
-                copy(by_z.at[i], z_arriving.at[z], zs_sem.at[i], zr_sem.at[z], dp, i * NC + c).start()
+                copy(by_z.at[i], z_arriving.at[z], zs_sem, zr_sem, dp, i * NC + c).start()
 
             @pl.when(i != y)
             def _():
-                copy(by_y.at[i], y_arriving.at[y], ys_sem.at[i], yr_sem.at[y], i * NX + x, vo).start()
+                copy(by_y.at[i], y_arriving.at[y], ys_sem, yr_sem, i * NX + x, vo).start()
 
             return carry
 
@@ -132,7 +132,7 @@
 
     def send_x(g, by_x, arriving, s_sem, r_sem):
         for k in (1, 2, 3):
-            copy(by_x.at[g, xp(k)], arriving.at[g, x], s_sem.at[g, k], r_sem.at[g, x], at_x(k), vo).start()
+            copy(by_x.at[g, xp(k)], arriving.at[g, x], s_sem, r_sem.at[g], at_x(k), vo).start()
 
     onehot = lax.broadcasted_iota(jnp.int32, (ROWS, TOKENS), 0) == labels[...] - (dp * LINE + vo) * ROWS
 
@@ -148,7 +148,7 @@
     def _():
         hb0[dp] = hidden[:, 0:SHARE]
         for k in (1, 2, 3):
-            copy(hb0.at[dp], hb0.at[dp], hs.at[k], hr.at[dp], at_x(k), vo).start()
+            copy(hb0.at[dp], hb0.at[dp], hs.at[0], hr.at[dp], at_x(k), vo).start()
         w_copy.wait()
         transpose_head(0, 18)
         for k in (1, 2, 3):
@@ -157,38 +157,36 @@
         def row(k):
             return hb0.at[pl.ds(yp(k) * NX, NX)]
 
-        def row_copy(from_k, to_k, sem):
-            return copy(row(from_k), row(from_k), hs.at[sem], hr.at[yp(from_k) * NX], at_y(to_k), vo)
+        def row_copy(from_k, to_k):
+            return copy(row(from_k), row(from_k), hs.at[1], hr.at[yp(from_k) * NX], at_y(to_k), vo)
 
         def across(k):
-            copy(row(k), row(k), hds.at[yp(k)], hdr.at[yp(k)], dp, sib).start()
+            copy(row(k), row(k), hds, hdr, dp, sib).start()
 
         def row_got(k):
             got(row(k), hr.at[yp(k) * NX])
 
-        row_copy(0, 1, 4).start()
-        row_copy(0, -1, 5).start()
-        row_copy(0, 4, 6).start()
+        row_copy(0, 1).start()
+        row_copy(0, -1).start()
+        row_copy(0, 4).start()
         across(0)
         label_first()
         row_got(-1)
-        row_copy(-1, 1, 7).start()
+        row_copy(-1, 1).start()
         row_got(1)
-        row_copy(1, -1, 8).start()
+        row_copy(1, -1).start()
         across(-1)
         across(1)
         label_second()
         row_got(4)
-        row_copy(4, 1, 9).start()
-        row_copy(4, -1, 10).start()
+        row_copy(4, 1).start()
+        row_copy(4, -1).start()
         across(4)
         for k in (2, -2, 3, -3):
             row_got(k)
             across(k)
-        for k in (1, 2, 3):
-            sent(hb0.at[dp], hs.at[k])
-        for sem in range(4, 11):
-            sent(row(0), hs.at[sem])
+        sent(hb0.at[pl.ds(0, 3)], hs.at[0])
+        sent(hb0.at[pl.ds(0, 28)], hs.at[1])
 
     @pl.when(c == 1)
     def _():
@@ -199,10 +197,10 @@
 
         def spread(k):
             for i in (1, 2, 3):
-                copy(own(k), own(k), hs.at[7 + yp(k) * 3 + i], hr.at[at_y(k)], yp(0) * NX + xp(i), vo).start()
+                copy(own(k), own(k), hs.at[1], hr.at[at_y(k)], yp(0) * NX + xp(i), vo).start()
 
         for k in (1, -1, 2, -2, 3, -3, 4):
-            copy(own(0), own(0), hs.at[yp(k)], hr.at[dp], at_y(k), vo).start()
+            copy(own(0), own(0), hs.at[0], hr.at[dp], at_y(k), vo).start()
         spread(0)
         w_copy.wait()
         transpose_head(0, 18)
@@ -220,21 +218,15 @@
                 slot = yp(k) * NX + xp(i)
                 got(hb1.at[slot], hr.at[slot])
             rows = hb1.at[pl.ds(yp(k) * NX, NX)]
-            copy(rows, rows, hds.at[yp(k)], hdr.at[yp(k)], dp, sib).start()
-        for k in (1, -1, 2, -2, 3, -3, 4):
-            sent(own(0), hs.at[yp(k)])
-        for k in range(8, 32):
-            sent(own(0), hs.at[k])
+            copy(rows, rows, hds, hdr, dp, sib).start()
+        sent(hb1.at[pl.ds(0, 7)], hs.at[0])
+        sent(hb1.at[pl.ds(0, 24)], hs.at[1])
 
     for g in range(2):
         send_x(g, bpx, brx, bxs, bxr)
     def across_done(sending, arriving):
-        def body(v, carry):
-            got(arriving.at[pl.ds(v * NX, NX)], hdr.at[v])
-            sent(sending.at[pl.ds(v * NX, NX)], hds.at[v])
-            return carry
-
-        lax.fori_loop(0, NY, body, 0)
+        got(arriving, hdr)
+        sent(sending, hds)
 
     pl.when(c == 0)(lambda: across_done(hb0, hb1))
     pl.when(c == 1)(lambda: across_done(hb1, hb0))
@@ -250,46 +242,45 @@
     terms = jnp.exp(softcap * squash)
 
     slope = 1.0 - squash * squash
-    den_a[vo] = jnp.concatenate([
+    den_b[dp] = jnp.concatenate([
         jnp.sum(terms, axis=0, keepdims=True),
         jnp.sum(jnp.where(onehot, terms, 0.0), axis=0, keepdims=True),
         jnp.sum(jnp.where(onehot, slope, 0.0), axis=0, keepdims=True)], axis=1)
-    each(LINE, lambda k: copy(
-        den_a.at[vo], den_a.at[vo], das.at[k], dar.at[vo], dp, lax.rem(vo + k, LINE)).start())
+    each(PLANE, lambda k: copy(
+        den_b.at[dp], den_b.at[dp], dbs, dbr, lax.rem(dp + k, PLANE), vo).start())
     lt[0:ROWS, :] = jnp.where(onehot, 0.0, terms * slope).astype(bf16)
     for_sibling(lt, ds_, dr_, c_s, c_r)
     for g in range(2):
         own_half(g, lt, dr_, c_r, px, pz, rz, zs, zr, py, r1y, y1s, y1r)
         send_x(g, px, rx, xs, xr)
-    each(LINE, lambda k: got(den_a.at[vo], dar.at[lax.rem(vo + k, LINE)]))
-    each(LINE, lambda k: sent(den_a.at[vo], das.at[k]))
-    den_b[dp] = jnp.sum(den_a[...], axis=0)
-    each(PLANE, lambda k: copy(
-        den_b.at[dp], den_b.at[dp], dbs.at[k], dbr.at[dp], lax.rem(dp + k, PLANE), vo).start())
+    got(den_b.at[pl.ds(0, PLANE - 1)], dbr)
+    den_a[vo] = jnp.sum(den_b[...], axis=0)
+    each(LINE, lambda k: copy(
+        den_a.at[vo], den_a.at[vo], das, dar, dp, lax.rem(vo + k, LINE)).start())
 
     def summed(own, arriving, count, at, recv):
         total = own.astype(f32)
+        got(arriving.at[pl.ds(0, count - 1)], recv)
         for k in range(1, count):
-            got(arriving.at[0], recv.at[at(k)])
             total += arriving[at(k)].astype(f32)
         return total
 
     def x_sum(g, own, arriving, recv):
         total = own[g, x].astype(f32)
+        got(arriving.at[g, pl.ds(0, 3)], recv.at[g])
         for k in (1, 2, 3):
-            got(arriving.at[g, 0], recv.at[g, xp(k)])
             total += arriving[g, xp(k)].astype(f32)
         return total.astype(bf16)
 
     def over_x(rows, arriving, s_sem, r_sem):
         for k in (1, 2, 3):
-            copy(rows.at[xp(k)], arriving.at[x], s_sem.at[k], r_sem.at[x], at_x(k), vo).start()
+            copy(rows.at[xp(k)], arriving.at[x], s_sem, r_sem, at_x(k), vo).start()
 
     def over_z(g, rows, arriving, s_sem, r_sem):
         def body(i, carry):
             @pl.when(i != z)
             def _():
-                copy(rows.at[i], arriving.at[z], s_sem.at[i], r_sem.at[z], dp, i * NC + c).start()
+                copy(rows.at[i], arriving.at[z], s_sem, r_sem, dp, i * NC + c).start()
 
             return carry
 
@@ -312,9 +303,8 @@
     label[LXU:XU + ZU] = summed(bqz[x], br2z, NX, xp, bz2r).astype(bf16)
     label[0:LXU] = summed(bqx[z], br2x, NZ, zp, bx2r).astype(bf16)
 
-    each(PLANE, lambda k: got(den_b.at[dp], dbr.at[lax.rem(dp + k, PLANE)]))
-    each(PLANE, lambda k: sent(den_b.at[dp], dbs.at[k]))
-    sums = jnp.sum(den_b[...], axis=0)
+    got(den_a.at[pl.ds(0, LINE - 1)], dar)
+    sums = jnp.sum(den_a[...], axis=0)
     inverse = 1.0 / sums[:, 0:TOKENS]
     at_label = ((sums[:, TOKENS:2 * TOKENS] * inverse - 1.0) * sums[:, 2 * TOKENS:]).astype(bf16).astype(f32)
 
@@ -325,24 +315,23 @@
 
     @pl.when(z != y)
     def _():
-        copy(sy, r3y.at[z], y3s, y3r.at[z], dp, y * NC + c).start()
+        copy(sy, r3y.at[z], y3s, y3r, dp, y * NC + c).start()
 
     ry[y, XU:] = joined(summed(qz[x], r2z, NX, xp, z2r), XU, XU + ZU)
     ry[y, 0:XU] = joined(summed(qx[z], r2x, NZ, zp, x2r), 0, XU)
 
-    each(NY, lambda k: copy(ry.at[y], ry.at[y], ys.at[k], yr.at[y], at_y(k), vo).start())
+    each(NY, lambda k: copy(ry.at[y], ry.at[y], ys, yr, at_y(k), vo).start())
 
     @pl.when(z == y)
     def _():
-        each(NZ, lambda k: got(r3y.at[0], y3r.at[zp(k)]))
+        got(r3y.at[pl.ds(0, NZ - 1)], y3r)
         done = sy[...].astype(f32)
         for k in range(1, NZ):
             done += r3y[zp(k)].astype(f32)
         yb[...] = done.astype(bf16)
-        each(NY, lambda k: copy(yb, yb, y4s.at[k], y4r, at_y(k), vo).start())
-
-    each(NY, lambda k: got(ry.at[0], yr.at[yp(k)]))
-    each(NY, lambda k: sent(ry.at[0], ys.at[k]))
+        each(NY, lambda k: copy(yb, yb, y4s, y4r, at_y(k), vo).start())
+
+    got(ry.at[pl.ds(0, NY - 1)], yr)
     total = ry[0].astype(f32)
     for k in range(1, NY):
         total += ry[k].astype(f32)
@@ -366,15 +355,15 @@
         def body(k, carry):
             @pl.when(jnp.logical_not(own_taker) | (k > 0))
             def _():
-                copy(quarter(x), rb, bs.at[k], br, taker_dp, zp(k) * NC + taker_core).start()
+                copy(quarter(x), rb, bs, br, taker_dp, zp(k) * NC + taker_core).start()
 
             return carry
 
         lax.fori_loop(0, NZ, body, 0)
 
     for k in (1, 2, 3):
-        copy(quarter(x), quarter(x), gs.at[k], gr.at[x], at_x(k), vo).start()
-    copy(quarter(x), quarter(x), gds.at[x], gdr.at[x], dp, sib).start()
+        copy(quarter(x), quarter(x), gs, gr.at[x], at_x(k), vo).start()
+    copy(quarter(x), quarter(x), gds, gdr.at[x], dp, sib).start()
 
     @pl.when(holds & own_taker)
     def _():
@@ -382,7 +371,7 @@
 
     for k in (1, 3, 2):
         got(quarter(xp(k)), gr.at[xp(k)])
-        copy(quarter(xp(k)), quarter(xp(k)), gds.at[xp(k)], gdr.at[xp(k)], dp, sib).start()
+        copy(quarter(xp(k)), quarter(xp(k)), gds, gdr.at[xp(k)], dp, sib).start()
 
     block = gb[pl.ds(shift, 36)].astype(f32).reshape(CHUNK, TOKENS).astype(bf16)
     token = lax.broadcasted_iota(jnp.int32, (8, TOKENS), 1)
@@ -413,7 +402,7 @@
 
         @pl.when(NZ * c + place != vo)
         def _():
-            copy(tb.at[place], rt.at[z], ts.at[place], tr.at[z], dp, NZ * c + place).start()
+            copy(tb.at[place], rt.at[z], ts, tr.at[z], dp, NZ * c + place).start()
 
         return carry
 
@@ -432,46 +421,42 @@
         at = v * NC * CHUNK // 128 * 128
         gram_rows[:, at:at + 640] += rt[v].astype(f32)[0:9]
 
-    def places_sent(place, carry):
-        @pl.when(NZ * c + place != vo)
-        def _():
-            sent(tb.at[0], ts.at[place])
-
-        @pl.when(holds & (jnp.logical_not(own_taker) | (place > 0)))
-        def _():
-            sent(rb, bs.at[place])
-
-        return carry
-
-    lax.fori_loop(0, NZ, places_sent, 0)
-    for v in range(NX):
-        sent(quarter(v), gds.at[v])
-    for k in (1, 2, 3):
-        sent(quarter(x), gs.at[k])
+    sent(tb.at[pl.ds(0, NZ - 1)], ts)
+
+    @pl.when(sender != c)
+    def _():
+        sent(tb.at[0], ts)
+
+    @pl.when(holds)
+    def _():
+        sent(gb.at[pl.ds(0, (NZ - 1) * UNITS)], bs)
+
+    @pl.when(holds & jnp.logical_not(own_taker))
+    def _():
+        sent(rb, bs)
+
+    sent(gb.at[pl.ds(0, NX * UNITS)], gds)
+    sent(gb.at[pl.ds(0, 3 * UNITS)], gs)
+    sent(ry.at[pl.ds(0, NY - 1)], ys)
+    sent(den_b.at[pl.ds(0, PLANE - 1)], dbs)
+    sent(den_a.at[pl.ds(0, LINE - 1)], das)
 
     @pl.when(z == y)
     def _():
-        each(NY, lambda k: sent(yb, y4s.at[k]))
+        sent(r3y.at[pl.ds(0, NY - 1)], y4s)
 
     @pl.when(z != y)
     def _():
         sent(sy, y3s)
 
-    each(NY, lambda k: sent(py.at[0], y1s.at[yp(k)]))
-    each(NY, lambda k: sent(bpy.at[0], by1s.at[yp(k)]))
-    each(NZ, lambda k: sent(pz.at[0], zs.at[zp(k)]))
-    each(NZ, lambda k: sent(bpz.at[0], bzs.at[zp(k)]))
-    each(NZ, lambda k: sent(qx.at[0], x2s.at[zp(k)]))
-    each(NZ, lambda k: sent(bqx.at[0], bx2s.at[zp(k)]))
-    for k in (1, 2, 3):
-        sent(qz.at[0], z2s.at[k])
-        sent(qy.at[0], y2s.at[k])
-        sent(bqz.at[0], bz2s.at[k])
-        sent(bqy.at[0], by2s.at[k])
-        for g in range(2):
-            sent(px.at[g, 0], xs.at[g, k])
-            sent(bpx.at[g, 0], bxs.at[g, k])
-    lax.fori_loop(0, NZ, lambda i, carry: (sent(ds_.at[i], c_s.at[i]), sent(bds.at[i], bc_s.at[i]), carry)[2], 0)
+    for rows, sem in ((py, y1s), (bpy, by1s), (pz, zs), (bpz, bzs), (qx, x2s), (bqx, bx2s)):
+        sent(rows.at[pl.ds(0, NZ - 1)], sem)
+    for rows, sem in ((qz, z2s), (qy, y2s), (bqz, bz2s), (bqy, by2s)):
+        sent(rows.at[pl.ds(0, NX - 1)], sem)
+    for rows, sem in ((px, xs), (bpx, bxs)):
+        sent(rows.at[:, pl.ds(0, NX - 1)], sem)
+    sent(ds_, c_s)
+    sent(bds, bc_s)
 
 
 def update(gram_rows, grads_in, factor, new_factor, grads):
@@ -514,13 +499,11 @@
             buf(YU, 8, TOKENS),
             buf(NZ, LXU, 8, TOKENS), buf(NX, LZU, 8, TOKENS), buf(NX, YU, 8, TOKENS),
             buf(NZ, LXU, 8, TOKENS), buf(NX, LZU, 8, TOKENS), buf(NX, YU, 8, TOKENS), buf(UNITS, 8, TOKENS),
-            dma, dma((2,)), dma((32,)), dma((32,)), dma((8,)), dma((8,)),
-            dma((LINE,)), dma((LINE,)), dma((PLANE,)), dma((PLANE,)), dma((NZ,)), dma((NZ,)),
-            dma((2, NX)), dma((2, NX)), dma((NZ,)), dma((NZ,)), dma((NZ,)), dma((NZ,)), dma((NX,)), dma((NX,)),
-            dma((NY,)), dma((NY,)), dma((NX,)), dma((NX,)), dma((NZ,)), dma, dma((NZ,)), dma((NZ,)), dma((NX,)), dma((NX,)),
-            dma((NZ,)), dma((NZ,)), dma((2, NX)), dma((2, NX)), dma((NZ,)), dma((NZ,)),
-            dma((NY,)), dma((NY,)), dma((NY,)), dma((NY,)), dma((NX,)), dma((NX,)), dma, dma((NZ,)), dma((NY,)), dma,
-            dma((NZ,)), dma((NZ,)), dma((NX,)), dma((NX,)), dma((NX,)), dma((NX,)),
+            dma, dma((2,)), dma((2,)), dma((32,)), dma, dma, dma, dma, dma, dma, dma, dma((NZ,)),
+            dma, dma((2,)), dma, dma, dma, dma, dma, dma, dma, dma, dma, dma((NX,)),
+            dma, dma, dma, dma((NZ,)), dma, dma((NX,)), dma, dma((NZ,)), dma, dma((2,)), dma, dma,
+            dma, dma, dma, dma, dma, dma, dma, dma, dma, dma, dma, dma,
+            dma, dma, dma, dma,
         ],
         compiler_params=pltpu.CompilerParams(
             collective_id=0, has_side_effects=True, vmem_limit_bytes=56 * 2**20),

time: 83.7 us -> 79.7 us (0.952); the launches traced: 82 us -> 79.3 us
  Pallas kernels: 81.4 us -> 78.7 us
    pallas_call x1, Pallas kernels: 79.5 us -> 76.9 us  [on_device(): pl.pallas_call(kernel, out_shape=(jax.ShapeDtypeStruct(factor_rows.shape,...]
where the time goes in v5:
time: 79.7 us; the launch traced here: 79.3 us
  Pallas kernels  78.7 us (99%)
    pallas_call x1, Pallas kernels, on_device(): pl.pallas_call(kernel, out_shape=(jax.ShapeDtypeStruct(factor_rows.shape,...  76.9 us
    pallas_call x1, Pallas kernels, on_device(): pl.pallas_call(update, out_shape=(jax.ShapeDtypeStruct(factor_rows.shape,...  1.84 us

profile of v5, /device:TPU:1, one launch (start us, length us, event | category | flops | bytes accessed | tf_op | source)
XLA Modules:
  0.0 79.3 jit_solution(10720809881018121904)
XLA Ops:
  0.6 76.9 %shard_map.59 = (f32[9,4608]{1,0:T(8,128)}, bf16[8,288]{1,0:T(8,128)(2,1)}) custom-call(bf16[8,4608]{1,0:T(8,128)(2,1)} %hidden_in.1, s32[1,256]{1,0:T(1,128)} %bitcast.1, bf16[500,4608]{1,0:T(8,128)(2,1)} %head.1), custom_call_target="tpu_custom_call" | custom-call | flops 2359296000 | bytes 6291456 | tf_op jit(solution)/shard_map/pallas_call | solution.py:476
  77.5 1.8 %shard_map.60 = (f32[9,4608]{1,0:T(8,128)}, bf16[8,288]{1,0:T(8,128)(2,1)}) custom-call(f32[9,4608]{1,0:T(8,128)} %get-tuple-element.4.gram_rows, bf16[8,288]{1,0:T(8,128)(2,1)} %get-tuple-element.5.grads_in, f32[9,4608]{1,0:T(8,128)} %factor.1), custom_call_target="tpu_custom_call" | custom-call | tf_op jit(solution)/shard_map/pallas_call | solution.py:512

commit v6 on v5

--- a/solution.py
+++ b/solution.py
@@ -25,7 +25,7 @@
     hidden_in, labels_in, head, gram_rows, grads,
     hidden, labels, wv, wt, hb0, hb1, h2, lt, ds_, dr_, px, pz, rx, rz, qx, qz, r2x, r2z, ry, gb, rb, tb, rt, den_a, den_b, lab, bds, bdr, bpx, bpz, brx, brz,
     py, r1y, bpy, br1y, qy, r2y, sy, r3y, yb,
-    bqx, bqz, bqy, br2x, br2z, br2y, label,
+    bqx, bqz, bqy, br2x, br2z, br2y, label, logits,
     w_sem, in_sem, hs, hr, hds, hdr, das, dar, dbs, dbr, c_s, c_r, xs, xr, zs, zr, x2s, x2r, z2s, z2r,
     ys, yr, gs, gr, bs, br, ts, tr, gds, gdr, bc_s, bc_r, bxs, bxr, bzs, bzr,
     y1s, y1r, by1s, by1r, y2s, y2r, y3s, y3r, y4s, y4r, bx2s, bx2r, bz2s, bz2r, by2s, by2r,
@@ -224,20 +224,30 @@
 
     for g in range(2):
         send_x(g, bpx, brx, bxs, bxr)
-    def across_done(sending, arriving):
-        got(arriving, hdr)
-        sent(sending, hds)
-
-    pl.when(c == 0)(lambda: across_done(hb0, hb1))
-    pl.when(c == 1)(lambda: across_done(hb1, hb0))
-
-    raw = jnp.zeros((ROWS, TOKENS), f32)
-    for part, block in enumerate((hb0, hb1, hb1, hb1)):
-        at = part * SHARE
-        skip = max(at - SHARE, 0)
-        h2[...] = block[:, :, skip:skip + SHARE].astype(f32).reshape(TOKENS, SHARE).astype(bf16)
-        raw += lax.dot_general(
-            wv[:, at:at + SHARE], h2[...], (((1,), (1,)), ((), ())), preferred_element_type=f32)
+
+    def logits_of(block, first):
+        total = None
+        for part in range(block.shape[2] // SHARE):
+            at = first + part * SHARE
+            h2[...] = block[:, :, part * SHARE:(part + 1) * SHARE].astype(f32).reshape(TOKENS, SHARE).astype(bf16)
+            product = lax.dot_general(
+                wv[:, at:at + SHARE], h2[...], (((1,), (1,)), ((), ())), preferred_element_type=f32)
+            total = product if total is None else total + product
+        return total
+
+    @pl.when(c == 0)
+    def _():
+        logits[...] = logits_of(hb0, 0)
+        got(hb1, hdr)
+        logits[...] += logits_of(hb1, SHARE)
+
+    @pl.when(c == 1)
+    def _():
+        logits[...] = logits_of(hb1, SHARE)
+        got(hb0, hdr)
+        logits[...] += logits_of(hb0, 0)
+
+    raw = logits[...]
     squash = jnp.tanh(raw * (1.0 / softcap))
     terms = jnp.exp(softcap * squash)
 
@@ -420,6 +430,14 @@
 
         at = v * NC * CHUNK // 128 * 128
         gram_rows[:, at:at + 640] += rt[v].astype(f32)[0:9]
+
+    @pl.when(c == 0)
+    def _():
+        sent(hb0, hds)
+
+    @pl.when(c == 1)
+    def _():
+        sent(hb1, hds)
 
     sent(tb.at[pl.ds(0, NZ - 1)], ts)
 
@@ -498,7 +516,7 @@
             buf(NX, YU, 8, TOKENS), buf(NX, YU, 8, TOKENS), buf(YU, 8, TOKENS), buf(NZ, YU, 8, TOKENS),
             buf(YU, 8, TOKENS),
             buf(NZ, LXU, 8, TOKENS), buf(NX, LZU, 8, TOKENS), buf(NX, YU, 8, TOKENS),
-            buf(NZ, LXU, 8, TOKENS), buf(NX, LZU, 8, TOKENS), buf(NX, YU, 8, TOKENS), buf(UNITS, 8, TOKENS),
+            buf(NZ, LXU, 8, TOKENS), buf(NX, LZU, 8, TOKENS), buf(NX, YU, 8, TOKENS), buf(UNITS, 8, TOKENS), buf(ROWS, TOKENS, dtype=f32),
             dma, dma((2,)), dma((2,)), dma((32,)), dma, dma, dma, dma, dma, dma, dma, dma((NZ,)),
             dma, dma((2,)), dma, dma, dma, dma, dma, dma, dma, dma, dma, dma((NX,)),
             dma, dma, dma, dma((NZ,)), dma, dma((NX,)), dma, dma((NZ,)), dma, dma((2,)), dma, dma,

time: 79.7 us -> 78.8 us (0.989)
  Pallas kernels: 78.7 us -> 77.2 us
    pallas_call x1, Pallas kernels: 76.9 us -> 75.4 us  [on_device(): pl.pallas_call(kernel, out_shape=(jax.ShapeDtypeStruct(factor_rows.shape,...]
where the time goes in v6:
time: 78.8 us; the launch traced here: 77.8 us
  Pallas kernels  77.2 us (98%)
    pallas_call x1, Pallas kernels, on_device(): pl.pallas_call(kernel, out_shape=(jax.ShapeDtypeStruct(factor_rows.shape,...  75.4 us
    pallas_call x1, Pallas kernels, on_device(): pl.pallas_call(update, out_shape=(jax.ShapeDtypeStruct(factor_rows.shape,...  1.84 us

profile of v6, /device:TPU:1, one launch (start us, length us, event | category | flops | bytes accessed | tf_op | source)
XLA Modules:
  0.0 77.8 jit_solution(1068177120218347477)
XLA Ops:
  0.6 75.4 %shard_map.59 = (f32[9,4608]{1,0:T(8,128)}, bf16[8,288]{1,0:T(8,128)(2,1)}) custom-call(bf16[8,4608]{1,0:T(8,128)(2,1)} %hidden_in.1, s32[1,256]{1,0:T(1,128)} %bitcast.1, bf16[500,4608]{1,0:T(8,128)(2,1)} %head.1), custom_call_target="tpu_custom_call" | custom-call | flops 2359296000 | bytes 6291456 | tf_op jit(solution)/shard_map/pallas_call | solution.py:494
  76.0 1.8 %shard_map.60 = (f32[9,4608]{1,0:T(8,128)}, bf16[8,288]{1,0:T(8,128)(2,1)}) custom-call(f32[9,4608]{1,0:T(8,128)} %get-tuple-element.4.gram_rows, bf16[8,288]{1,0:T(8,128)(2,1)} %get-tuple-element.5.grads_in, f32[9,4608]{1,0:T(8,128)} %factor.1), custom_call_target="tpu_custom_call" | custom-call | tf_op jit(solution)/shard_map/pallas_call | solution.py:530
